TPU v7x, 512 devices: a whole 4x8x8 slice. The times are simulated.
512 devices in a mesh: dp: 64 (over z, y), mp: 8 (over x, core).
Axes of the slice: x: 4, y: 8, z: 8, core: 2. Of those that a mesh axis runs over, the one named last changes fastest.
Arguments:
- hidden_in: bfloat16 [8192, 4096], P('dp', 'mp'), may hold values from -100 to 100
- queries: bfloat16 [8192, 4096], P('dp', 'mp'), may hold values from -100 to 100
- image_kv: bfloat16 [128, 2, 32, 4096], P('dp', None, None, 'mp'), may hold values from -6 to 6
- image_owner: int32 [128], replicated, may hold values from 0 to 127, as said below
- citations: int32 [64, 32], replicated, may hold values from 0 to 127, as said below
- cite_mask: int32 [8192, 32], P('dp'), may hold values from 0 to 1, as said below
- gate_scalars: float32 [1], replicated, may hold values from 0.3 to 1.2
- norm_gain: float32 [4096], replicated, may hold values from 0.5 to 1.5
- upstream: bfloat16 [8192, 4096], P('dp', 'mp'), may hold values from -100 to 100
Outputs:
- block_out: bfloat16 [8192, 4096], P('dp', 'mp')
- normed_out: bfloat16 [8192, 4096], P('dp', 'mp')
- hidden_grad: bfloat16 [8192, 4096], P('dp', 'mp')
- query_grad: bfloat16 [8192, 4096], P('dp', 'mp')
- image_kv_grad: bfloat16 [128, 2, 32, 4096], P('dp', None, None, 'mp')
Inputs may be any that keep to these rules, and one draw needn't show every extreme that they name: `image_owner`: a permutation of the 128 rows of image_kv. `citations`: each row names 32 different image ids, and no two of them are stored by the same encoder shard (image_owner[id] // 2 differ). `cite_mask`: every text token has at least one 1.
All inputs are finite; a program needn't handle non-finite values.
Results may differ from a plain program's by a relative error of at most 0.0095.
Values may be sent and summed in bfloat16 or wider, within the bound.
A program may use at most 64 MiB of HBM per device.

v0:
```python
import jax
import jax.numpy as jnp
from jax import lax
from jax.sharding import PartitionSpec as P

D = 4096
HEAD_DIM = 128
IT = 32
IMG_DEV = 2


def local(
    hidden_in,
    queries,
    image_kv,
    image_owner,
    citations,
    cite_mask,
    gate_scalars,
    norm_gain,
    upstream,
):
    rows = hidden_in.shape[0]
    local_width = hidden_in.shape[1]
    heads_here = local_width // HEAD_DIM
    cites_here = cite_mask.shape[1]
    shards = citations.shape[0]
    column = lax.axis_index("mp")
    my_shard = lax.axis_index("dp")
    stored_all = image_owner[citations]
    owner_all = stored_all // IMG_DEV
    slot_all = stored_all % IMG_DEV
    my_stored = lax.dynamic_index_in_dim(stored_all, my_shard, 0, keepdims=False)
    sources = my_stored // IMG_DEV
    matches = owner_all == my_shard
    slot_range = jnp.arange(IMG_DEV, dtype=jnp.int32)
    serve = jnp.any(
        matches[:, :, None] & (slot_all[:, :, None] == slot_range[None, None, :]), axis=1
    )
    serve_low = serve.astype(jnp.bfloat16)
    item_size = 2 * IT * local_width
    stored_flat = image_kv.reshape(IMG_DEV, item_size)
    outgoing = jnp.dot(serve_low, stored_flat, preferred_element_type=jnp.float32).astype(
        jnp.bfloat16
    )
    outgoing = outgoing.reshape(shards, 2, IT, local_width)
    arrived = lax.all_to_all(outgoing, "dp", split_axis=0, concat_axis=0, tiled=True)
    selected = arrived[sources]
    key_heads = selected[:, 0].reshape(cites_here * IT, heads_here, HEAD_DIM).transpose(1, 0, 2)
    value_heads = selected[:, 1].reshape(cites_here * IT, heads_here, HEAD_DIM).transpose(1, 0, 2)
    query_heads = queries.reshape(rows, heads_here, HEAD_DIM).transpose(1, 0, 2)
    allowed = jnp.broadcast_to(cite_mask[:, :, None] > 0, (rows, cites_here, IT)).reshape(
        rows, cites_here * IT
    )
    scale = HEAD_DIM ** (-0.5)

    def head_probs(query_one, key_one):
        scores = (
            jnp.einsum("td,kd->tk", query_one, key_one, preferred_element_type=jnp.float32) * scale
        )
        scores = jnp.where(allowed, scores, jnp.float32(-1e30))
        return jax.nn.softmax(scores, axis=-1)

    def head_forward(item):
        query_one, key_one, value_one = item
        probs_low = head_probs(query_one, key_one).astype(jnp.bfloat16)
        return jnp.einsum("tk,kd->td", probs_low, value_one, preferred_element_type=jnp.float32)

    attended = lax.map(head_forward, (query_heads, key_heads, value_heads))
    attended = attended.transpose(1, 0, 2).reshape(rows, local_width)
    gate_attn = jnp.tanh(gate_scalars[0])
    block_out = (hidden_in.astype(jnp.float32) + gate_attn * attended).astype(jnp.bfloat16)
    local_mixed = block_out.astype(jnp.float32)
    local_gain = lax.dynamic_slice_in_dim(norm_gain, column * local_width, local_width)
    weighted = local_gain * upstream.astype(jnp.float32)
    square_part = jnp.sum(local_mixed * local_mixed, axis=-1)
    inner_part = jnp.sum(weighted * local_mixed, axis=-1)
    square_total = lax.psum(square_part, "mp")
    inverse = lax.rsqrt(square_total / D + 1e-05)[:, None]
    normed_out = (local_mixed * inverse * local_gain).astype(jnp.bfloat16)
    inner = lax.psum(inner_part, "mp")
    hidden_total = inverse * weighted - local_mixed * inverse**3 * inner[:, None] / D
    hidden_grad = hidden_total.astype(jnp.bfloat16)
    out_grad = (gate_attn * hidden_total).astype(jnp.bfloat16)
    grad_heads = out_grad.reshape(rows, heads_here, HEAD_DIM).transpose(1, 0, 2)

    def head_backward(item):
        query_one, key_one, value_one, grad_one = item
        probs = head_probs(query_one, key_one)
        probs_low = probs.astype(jnp.bfloat16)
        prob_grad = jnp.einsum("td,kd->tk", grad_one, value_one, preferred_element_type=jnp.float32)
        score_grad = (
            probs * (prob_grad - jnp.sum(probs * prob_grad, axis=-1, keepdims=True)) * scale
        ).astype(jnp.bfloat16)
        query_part = jnp.einsum(
            "tk,kd->td", score_grad, key_one, preferred_element_type=jnp.float32
        ).astype(jnp.bfloat16)
        key_part = jnp.einsum(
            "tk,td->kd", score_grad, query_one, preferred_element_type=jnp.float32
        ).astype(jnp.bfloat16)
        value_part = jnp.einsum(
            "tk,td->kd", probs_low, grad_one, preferred_element_type=jnp.float32
        ).astype(jnp.bfloat16)
        return (query_part, key_part, value_part)

    query_parts, key_parts, value_parts = lax.map(
        head_backward, (query_heads, key_heads, value_heads, grad_heads)
    )
    query_grad = query_parts.transpose(1, 0, 2).reshape(rows, local_width)
    key_grad = key_parts.transpose(1, 0, 2).reshape(cites_here, IT, local_width)
    value_grad = value_parts.transpose(1, 0, 2).reshape(cites_here, IT, local_width)
    cited_grad = jnp.stack([key_grad, value_grad], axis=1).reshape(cites_here, item_size)
    placing = (sources[None, :] == jnp.arange(shards, dtype=jnp.int32)[:, None]).astype(
        jnp.bfloat16
    )
    sendback = jnp.dot(placing, cited_grad, preferred_element_type=jnp.float32).astype(jnp.bfloat16)
    sendback = sendback.reshape(shards, 2, IT, local_width)
    returned = lax.all_to_all(sendback, "dp", split_axis=0, concat_axis=0, tiled=True)
    summed = jnp.dot(
        serve_low.T, returned.reshape(shards, item_size), preferred_element_type=jnp.float32
    )
    image_kv_grad = summed.astype(jnp.bfloat16).reshape(IMG_DEV, 2, IT, local_width)
    return (block_out, normed_out, hidden_grad, query_grad, image_kv_grad)


def solution(mesh):
    placed = (
        P("dp", "mp"),
        P("dp", "mp"),
        P("dp", None, None, "mp"),
        P(),
        P(),
        P("dp", None),
        P(),
        P(),
        P("dp", "mp"),
    )
    return jax.shard_map(
        local,
        mesh=mesh,
        in_specs=placed,
        out_specs=(
            P("dp", "mp"),
            P("dp", "mp"),
            P("dp", "mp"),
            P("dp", "mp"),
            P("dp", None, None, "mp"),
        ),
        check_vma=False,
    )
```

profile of v0, /device:TPU:114, one launch (start us, length us, event | category | flops | bytes accessed | tf_op | source)
XLA Modules:
  0.0 366.7 jit_solution(1976684595508803783)
XLA Ops:
  1.6 12.6 %gather_fusion = s32[2048]{0:T(1024)S(1)} fusion(s32[128]{0:T(128)S(1)} %copy-done, s32[2048]{0:T(1024)S(1)} %broadcast_clamp_fusion), kind=kCustom, calls=%fused_computation | custom fusion | bytes 24576 | tf_op jit(solution)/shard_map/gather | solution.py:30
  14.6 1.3 convolution_convert_fusion.4
  15.9 3.6 copy.99
  19.5 15.4 %all-to-all-start = ((bf16[64,2,32,512]{3,2,1,0:T(8,128)(2,1)}), bf16[64,2,32,512]{3,2,1,0:T(8,128)(2,1)}, u32[]{:S(2)}, u32[]{:S(2)}) async-start(bf16[64,2,32,512]{3,2,1,0:T(8,128)(2,1)} %bitcast.167), calls=%async_computation | async-start | bytes 8388608 | tf_op jit(solution)/shard_map/all_to_all | solution.py:47
  37.3 126.0 %all-to-all-done = bf16[64,2,32,512]{3,2,1,0:T(8,128)(2,1)} async-done(((bf16[64,2,32,512]{3,2,1,0:T(8,128)(2,1)}), bf16[64,2,32,512]{3,2,1,0:T(8,128)(2,1)}, u32[]{:S(2)}, u32[]{:S(2)}) %all-to-all-start) | async-done | bytes 4194336 | tf_op jit(solution)/shard_map/all_to_all | solution.py:47
  163.3 2.9 gather_fusion.1
  166.2 1.2 fusion.69
  167.4 1.3 reshape_squeeze.6
  169.4 7.0 %while.26 = (s32[]{:T(128)}, f32[4,128,128]{2,1,0:T(8,128)}, bf16[4,128,128]{2,1,0:T(8,128)(2,1)S(1)}, bf16[4,1024,128]{2,1,0:T(8,128)(2,1)S(1)}, bf16[4,1024,12...) while((s32[]{:T(128)}, f32[4,128,128]{2,1,0:T(8,128)}, ...), condition=%wide.region_4.5_spmd.clone, body=%wide.region_1.4_spmd.clone.sunk | while | flops 68157184 | bytes 2728533 | solution.py:69
  176.4 1.7 fusion.54
  178.1 11.4 %all-reduce = (f32[128]{0:T(128)}, f32[128]{0:T(128)}) all-reduce(f32[128]{0:T(128)} %get-tuple-element.187, f32[128]{0:T(128)} %get-tuple-element.186), channel_id=1, replica_groups=mesh['dp'=64,'mp'=8] {'mp'}, use_global_device_ids=true, to_apply=%region_6.7 | all-reduce | flops 256 | bytes 2048 | tf_op jit(solution)/shard_map/psum | solution.py:78
  190.1 1.5 fusion.57
  191.7 14.5 %while.27 = (s32[]{:T(128)}, bf16[4,128,128]{2,1,0:T(8,128)(2,1)}, bf16[4,1024,128]{2,1,0:T(8,128)(2,1)}, bf16[4,1024,128]{2,1,0:T(8,128)(2,1)S(1)}, bf16[4,128,...) while((s32[]{:T(128)}, bf16[4,128,128]{2,1,0:T(8,128)(2,1)}, ...), condition=%wide.region_13.14_spmd.clone, body=%wide.region_9.13_spmd.clone.sunk | while | flops 170409600 | bytes 6470253 | solution.py:106
  194.0 1.0 fusion.106
  197.6 1.0 fusion.106
  201.2 1.0 fusion.106
  204.9 1.0 fusion.106
  207.5 2.0 copy.92
  210.3 1.2 copy.100
  211.5 1.2 convolution_convert_fusion.3
  212.7 3.6 copy.101
  216.4 8.6 %all-to-all-start.1 = ((bf16[64,2,32,512]{3,2,1,0:T(8,128)(2,1)}), bf16[64,2,32,512]{3,2,1,0:T(8,128)(2,1)}, u32[]{:S(2)}, u32[]{:S(2)}) async-start(bf16[64,2,32,512]{3,2,1,0:T(8,128)(2,1)} %bitcast.168), calls=%async_computation.1 | async-start | bytes 8388608 | tf_op jit(solution)/shard_map/all_to_all | solution.py:118
  225.7 135.0 %all-to-all-done.1 = bf16[64,2,32,512]{3,2,1,0:T(8,128)(2,1)} async-done(((bf16[64,2,32,512]{3,2,1,0:T(8,128)(2,1)}), bf16[64,2,32,512]{3,2,1,0:T(8,128)(2,1)}, u32[]{:S(2)}, u32[]{:S(2)}) %all-to-all-start.1) | async-done | bytes 4194336 | tf_op jit(solution)/shard_map/all_to_all | solution.py:118
  360.7 4.7 %copy.102 = bf16[8,8,64,512]{3,1,2,0:T(8,128)(2,1)S(1)} copy(bf16[8,8,64,512]{3,2,1,0:T(8,128)(2,1)} %bitcast.48) | data formatting | bytes 8388608
  (104 shorter events, 25.5 us)
Async XLA Ops:
  0.6 0.9 copy-start
  1.5 12.8 %copy-start.4 = (bf16[2,2,32,512]{3,2,1,0:T(8,128)(2,1)S(1)}, bf16[2,2,32,512]{3,2,1,0:T(8,128)(2,1)}, u32[]{:S(2)}) copy-start(bf16[2,2,32,512]{3,2,1,0:T(8,128)(2,1)} %param.15) | copy-start | bytes 393220
  19.5 15.5 %copy-start.5 = (bf16[128,512]{1,0:T(8,128)(2,1)S(1)}, bf16[128,512]{1,0:T(8,128)(2,1)}, u32[]{:S(2)}) copy-start(bf16[128,512]{1,0:T(8,128)(2,1)} %param.14) | copy-start | bytes 393220
  19.5 17.8 %copy-start.7 = (s32[128,32]{0,1:T(8,128)S(1)}, s32[128,32]{0,1:T(8,128)}, u32[]{:S(2)}) copy-start(s32[128,32]{0,1:T(8,128)} %param.18) | copy-start | bytes 49156
  19.5 143.8 %all-to-all-start = ((bf16[64,2,32,512]{3,2,1,0:T(8,128)(2,1)}), bf16[64,2,32,512]{3,2,1,0:T(8,128)(2,1)}, u32[]{:S(2)}, u32[]{:S(2)}) async-start(bf16[64,2,32,512]{3,2,1,0:T(8,128)(2,1)} %bitcast.167), calls=%async_computation | async-start | bytes 8388608 | tf_op jit(solution)/shard_map/all_to_all | solution.py:47
  169.3 7.1 %copy-start.2 = (bf16[128,512]{1,0:T(8,128)(2,1)S(1)}, bf16[128,512]{1,0:T(8,128)(2,1)}, u32[]{:S(2)}) copy-start(bf16[128,512]{1,0:T(8,128)(2,1)} %param.21) | copy-start | bytes 393220
  169.3 22.4 %copy-start.1 = (bf16[4,1024,128]{2,1,0:T(8,128)(2,1)S(1)}, bf16[4,1024,128]{2,1,0:T(8,128)(2,1)}, u32[]{:S(2)}) copy-start(bf16[4,1024,128]{2,1,0:T(8,128)(2,1)} %custom-call.7) | copy-start | bytes 3145732
  178.1 13.6 %copy-start.3 = (bf16[128,512]{1,0:T(8,128)(2,1)}, bf16[128,512]{1,0:T(8,128)(2,1)S(1)}, u32[]{:S(2)}) copy-start(bf16[128,512]{1,0:T(8,128)(2,1)S(1)} %get-tuple-element.220) | copy-start | bytes 393220
  210.2 1.3 copy-start.8
  216.4 8.6 %copy-start.6 = (bf16[4,128,128]{2,1,0:T(8,128)(2,1)S(1)}, bf16[4,128,128]{2,1,0:T(8,128)(2,1)}, u32[]{:S(2)}) copy-start(bf16[4,128,128]{2,1,0:T(8,128)(2,1)} %get-tuple-element.87) | copy-start | bytes 393220
  216.4 144.3 %all-to-all-start.1 = ((bf16[64,2,32,512]{3,2,1,0:T(8,128)(2,1)}), bf16[64,2,32,512]{3,2,1,0:T(8,128)(2,1)}, u32[]{:S(2)}, u32[]{:S(2)}) async-start(bf16[64,2,32,512]{3,2,1,0:T(8,128)(2,1)} %bitcast.168), calls=%async_computation.1 | async-start | bytes 8388608 | tf_op jit(solution)/shard_map/all_to_all | solution.py:118
where the time goes:
time: 367 us
  waiting for transfers between devices  261 us (71%)
  local copies, waits for them, and re-layouts  40.5 us (11%)
  starting transfers between devices  24 us (7%)
  matrix products  19.6 us (5%)
  blocking collectives  11.4 us (3%)
  other arithmetic  8.34 us (2%)
    all_to_all x1, waiting for transfers between devices, local(): lax.all_to_all(sendback, 'dp', split_axis=0, concat_axis=0, tiled=True)  135 us
    all_to_all x1, waiting for transfers between devices, local(): lax.all_to_all(outgoing, 'dp', split_axis=0, concat_axis=0, tiled=True)  126 us
    all_to_all x1, starting transfers between devices, local(): lax.all_to_all(outgoing, 'dp', split_axis=0, concat_axis=0, tiled=True)  15.4 us
    unnamed x28, local copies, waits for them, and re-layouts  14.5 us
    gather x3, local copies, waits for them, and re-layouts, local(): stored_all = image_owner[citations]  12.8 us
    psum x1, blocking collectives, local(): square_total = lax.psum(square_part, 'mp')  11.4 us
    all_to_all x1, starting transfers between devices, local(): lax.all_to_all(sendback, 'dp', split_axis=0, concat_axis=0, tiled=True)  8.61 us
  transfers between devices with their start and end apart: 2, of which 2 were waited for; matrix products, arithmetic and copies ran while one was open for 1% of the time, Pallas kernels for 0%

commit v1 on v0

v1 whole, which is shorter than its diff:
```python
import functools

import jax
import jax.numpy as jnp
from jax import lax
from jax.experimental import pallas as pl
from jax.experimental.pallas import tpu as pltpu
from jax.sharding import PartitionSpec as P

HEAD_DIM = 128
IT = 32
IMG_DEV = 2
TOK = 128
Y = 8
G = 4
EPS = 1e-05
MESH = pl.DeviceIdType.MESH
F32 = jnp.float32
BF16 = jnp.bfloat16
NT = (((1,), (1,)), ((), ()))
TN = (((0,), (0,)), ((), ()))
NN = (((1,), (0,)), ((), ()))


def dot(left, right, dims):
    return lax.dot_general(left, right, dims, preferred_element_type=F32)


def kernel(
    Z,
    M,
    cites,
    rows_ref,
    pos_ref,
    gate_ref,
    hidden_ref,
    query_ref,
    kv_ref,
    bias_ref,
    gain_ref,
    upstream_ref,
    block_ref,
    normed_ref,
    hgrad_ref,
    qgrad_ref,
    kvgrad_ref,
    kv_all,
    q_all,
    bias_all,
    hid,
    ups,
    ksel,
    vsel,
    probs,
    att_out,
    att_in,
    stat_out,
    stat_in,
    mixed,
    normed,
    hgrad,
    og_out,
    og_in,
    dq_out,
    cited,
    sib_out,
    sib_in,
    rs_out,
    rs_in,
    fin_out,
    kv_s,
    kv_r,
    q_s,
    q_r,
    b_s,
    b_r,
    ag_s,
    ag_r,
    sa_s,
    sa_r,
    att_s,
    att_r,
    st_s,
    st_r,
    og_s,
    og_r,
    dq_s,
    dq_r,
    sr_s,
    sr_r,
    rs_s,
    rs_r,
    fin_s,
    fin_r,
    loc,
):
    T = Z // 2
    n_rows = Z * Y * IMG_DEV
    width = G * HEAD_DIM
    feats = M * width
    dp = lax.axis_index("dp")
    mp = lax.axis_index("mp")
    z, y = dp // Y, dp % Y
    x, core = mp // 2, mp % 2
    a, b = y // G, y % G
    right = lax.rem(z + 1, Z) * Y + y
    left = lax.rem(z + Z - 1, Z) * Y + y
    sibling = (dp, x * 2 + 1 - core)
    in_group = a == core

    def peer(i):
        return (z * Y + core * G + i, x * 2 + a)

    barrier = pltpu.get_barrier_semaphore()
    for k in range(1, M):
        pl.semaphore_signal(
            barrier, inc=1, device_id=(dp, lax.rem(mp + k, M)), device_id_type=MESH
        )
    for other in (left, right):
        pl.semaphore_signal(barrier, inc=1, device_id=(other, mp), device_id_type=MESH)
    for k in range(1, G):
        pl.semaphore_signal(
            barrier, inc=1, device_id=peer(lax.rem(b + k, G)), device_id_type=MESH
        )

    @pl.when(jnp.logical_not(in_group))
    def _():
        pl.semaphore_signal(barrier, inc=1, device_id=peer(b), device_id_type=MESH)

    hid_copy = pltpu.make_async_copy(hidden_ref, hid, loc.at[0])
    ups_copy = pltpu.make_async_copy(upstream_ref, ups, loc.at[1])
    hid_copy.start()
    ups_copy.start()

    pl.semaphore_wait(barrier, (M - 1) + 2 + (G - 1) + jnp.where(in_group, 0, 1))

    def remote(src, dst, ssem, rsem, device):
        return pltpu.make_async_remote_copy(
            src_ref=src,
            dst_ref=dst,
            send_sem=ssem,
            recv_sem=rsem,
            device_id=device,
            device_id_type=MESH,
        )

    def give(i, src, dst_of, ssem, rsem):
        mine = in_group & (i == b)

        @pl.when(mine)
        def _():
            pltpu.make_async_copy(src, dst_of(b), rsem.at[b]).start()

        @pl.when(jnp.logical_not(mine))
        def _():
            remote(src, dst_of(b), ssem.at[i], rsem.at[b], peer(i)).start()

    def take(i, dst_of, ssem, rsem):
        mine = in_group & (i == b)

        @pl.when(mine)
        def _():
            pltpu.make_async_copy(dst_of(i), dst_of(i), rsem.at[i]).wait()

        @pl.when(jnp.logical_not(mine))
        def _():
            remote(dst_of(i), dst_of(i), ssem.at[i], rsem.at[i], peer(i)).wait_recv()

    def given(i, src, ssem, rsem):
        mine = in_group & (i == b)

        @pl.when(jnp.logical_not(mine))
        def _():
            remote(src, src, ssem.at[i], rsem.at[i], peer(i)).wait_send()

    def head(i):
        return pl.ds(pl.multiple_of(i * HEAD_DIM, HEAD_DIM), HEAD_DIM)

    def kv_src(i):
        return kv_ref.at[:, :, :, head(i)]

    def piece(zb, yy):
        return kv_all.at[pl.ds((zb * Y + yy) * IMG_DEV, IMG_DEV)]

    def kv_dst(i):
        return piece(z, core * G + i)

    def kv_dst_at_peer(i):
        return piece(z, y)

    for k in range(G):
        i = lax.rem(b + k, G)
        give(i, kv_src(i), kv_dst_at_peer, kv_s, kv_r)
    for k in range(G):
        i = lax.rem(b + k, G)
        give(i, query_ref.at[:, head(i)], lambda j: q_all.at[j], q_s, q_r)
        give(i, bias_ref, lambda j: bias_all.at[j], b_s, b_r)

    def ring_copy(way, t, zb, i):
        block = piece(zb, core * G + i)
        return remote(
            block, block, ag_s.at[way, t, i], ag_r.at[way, t, i], (right if way == 0 else left, mp)
        )

    def half_block(zb):
        return kv_all.at[pl.ds((zb * Y + core * G) * IMG_DEV, G * IMG_DEV)]

    def other_half_block(zb):
        return kv_all.at[pl.ds((zb * Y + (1 - core) * G) * IMG_DEV, G * IMG_DEV)]

    def to_sibling(n, zb):
        remote(half_block(zb), half_block(zb), sa_s.at[n], sa_r.at[n], sibling).start()

    def from_way(way, t):
        return lax.rem(z + (Z - t if way == 0 else t), Z)

    def in_step(way, t, i):
        return t < T or (i < G // 2) == (way == 0)

    for i in range(G):
        take(i, kv_dst, kv_s, kv_r)
        for way in (0, 1):
            if in_step(way, 1, i):
                ring_copy(way, 0, z, i).start()
    to_sibling(0, z)
    for t in range(1, T + 1):
        for i in range(G):
            for way in (0, 1):
                if in_step(way, t, i):
                    zb = from_way(way, t)
                    ring_copy(way, t - 1, zb, i).wait_recv()
                    if t < T and in_step(way, t + 1, i):
                        ring_copy(way, t, zb, i).start()
        if t < T:
            to_sibling(2 * t - 1, from_way(0, t))
            to_sibling(2 * t, from_way(1, t))
        else:
            to_sibling(2 * t - 1, from_way(0, t))
    for n in range(Z):
        zb = from_way(n % 2 ^ 1, (n + 1) // 2)
        remote(other_half_block(zb), other_half_block(zb), sa_s.at[n], sa_r.at[n], sibling).wait_recv()
    for i in range(G):
        take(i, lambda j: q_all.at[j], q_s, q_r)
        take(i, lambda j: bias_all.at[j], b_s, b_r)

    scale = HEAD_DIM**-0.5
    log2e = 1.4426950408889634

    def forward(s, _):
        for n in range(cites):
            row = rows_ref[s * cites + n]
            ksel[s, n * IT : (n + 1) * IT] = kv_all[row, 0]
            vsel[s, n * IT : (n + 1) * IT] = kv_all[row, 1]
        scores = dot(ksel[s], q_all[s], NT) * (scale * log2e)
        scores = scores.reshape(cites, IT, TOK) + bias_all[s][:, None, :]
        top = jnp.max(jnp.max(scores, axis=0), axis=0, keepdims=True)
        weights = jnp.exp2(scores - top[None])
        total = jnp.sum(jnp.sum(weights, axis=0), axis=0, keepdims=True)
        weights = (weights * (1.0 / total)[None]).reshape(cites * IT, TOK)
        probs[s] = weights
        att_out[s] = dot(weights.astype(BF16), vsel[s], TN).astype(BF16)
        give(s, att_out.at[s], lambda j: att_in.at[j], att_s, att_r)
        return 0

    lax.fori_loop(0, G, forward, 0)

    gate = gate_ref[0]
    hid_copy.wait()
    ups_copy.wait()
    gain = gain_ref[pl.ds(mp, 1), :]
    square = jnp.zeros((TOK, HEAD_DIM), F32)
    inner = jnp.zeros((TOK, HEAD_DIM), F32)
    for i in range(G):
        take(i, lambda j: att_in.at[j], att_s, att_r)
        lanes = slice(i * HEAD_DIM, (i + 1) * HEAD_DIM)
        block = (hid[:, lanes].astype(F32) + gate * att_in[i].astype(F32)).astype(BF16)
        mixed[:, lanes] = block
        wide = block.astype(F32)
        square += wide * wide
        inner += gain[:, lanes] * ups[:, lanes].astype(F32) * wide
    block_copy = pltpu.make_async_copy(mixed, block_ref, loc.at[2])
    block_copy.start()
    lane = lax.broadcasted_iota(jnp.int32, (TOK, HEAD_DIM), 1)
    both = jnp.where(
        lane == 0, jnp.sum(square, axis=1, keepdims=True), jnp.sum(inner, axis=1, keepdims=True)
    )
    stat_out[...] = jnp.transpose(both)[:8]
    stat_in[mp] = stat_out[...]
    for k in range(1, M):
        other = lax.rem(mp + k, M)
        remote(stat_out, stat_in.at[mp], st_s.at[k], st_r.at[mp], (dp, other)).start()
    for k in range(1, M):
        other = lax.rem(mp + k, M)
        remote(stat_out, stat_in.at[other], st_s.at[k], st_r.at[other], (dp, other)).wait_recv()
    total = stat_in[0]
    for k in range(1, M):
        total += stat_in[k]
    columns = jnp.transpose(jnp.concatenate([total] * (TOK // 8), axis=0))
    inverse = lax.rsqrt(columns[:, 0:1] / feats + EPS)
    slope = inverse * inverse * inverse * columns[:, 1:2] / feats
    for i in range(G):
        lanes = slice(i * HEAD_DIM, (i + 1) * HEAD_DIM)
        wide = mixed[:, lanes].astype(F32)
        weighted = gain[:, lanes] * ups[:, lanes].astype(F32)
        grad = inverse * weighted - wide * slope
        og_out[i] = (gate * grad).astype(BF16)
        give(i, og_out.at[i], lambda j: og_in.at[j], og_s, og_r)
        hgrad[:, lanes] = grad.astype(BF16)
        normed[:, lanes] = (wide * inverse * gain[:, lanes]).astype(BF16)
    normed_copy = pltpu.make_async_copy(normed, normed_ref, loc.at[3])
    hgrad_copy = pltpu.make_async_copy(hgrad, hgrad_ref, loc.at[4])
    normed_copy.start()
    hgrad_copy.start()

    def qgrad_slot(j):
        return qgrad_ref.at[:, head(j)]

    def backward(s, _):
        take(s, lambda j: og_in.at[j], og_s, og_r)
        out_grad = og_in[s]
        weights = probs[s]
        prob_grad = dot(vsel[s], out_grad, NT)
        mean = jnp.sum(weights * prob_grad, axis=0, keepdims=True)
        score_grad = (weights * (prob_grad - mean) * scale).astype(BF16)
        dq_out[s] = dot(score_grad, ksel[s], TN).astype(BF16)
        give(s, dq_out.at[s], qgrad_slot, dq_s, dq_r)
        cited[s, :cites, 0] = dot(score_grad, q_all[s], NN).reshape(cites, IT, HEAD_DIM)
        cited[s, :cites, 1] = dot(weights.astype(BF16), out_grad, NN).reshape(cites, IT, HEAD_DIM)
        cited[s, cites] = jnp.zeros((2, IT, HEAD_DIM), F32)
        return 0

    lax.fori_loop(0, G, backward, 0)

    def part(zb, yy, image):
        row = (zb * Y + yy) * IMG_DEV + image
        total = cited[0, pos_ref[row]]
        for s in range(1, G):
            total += cited[s, pos_ref[s * n_rows + row]]
        return total

    def target(way, t):
        return lax.rem(z + (T - t if way == 0 else Z - T + t), Z)

    order = [target(0, 0)]
    for t in range(1, T):
        order += [target(0, t), target(1, t)]
    order += [z]
    for n, zb in enumerate(order):

        def for_sibling(i, _):
            for image in range(IMG_DEV):
                sib_out[n, i, image] = part(zb, (1 - core) * G + i, image).astype(BF16)
            return 0

        lax.fori_loop(0, G, for_sibling, 0)
        remote(sib_out.at[n], sib_in.at[n], sr_s.at[n], sr_r.at[n], sibling).start()

    def pass_on(way, t, i):
        return remote(
            rs_out.at[way, t, i],
            rs_in.at[way, t, i],
            rs_s.at[way, t, i],
            rs_r.at[way, t, i],
            (right if way == 0 else left, mp),
        )

    def sib_wait(n):
        remote(sib_out.at[n], sib_in.at[n], sr_s.at[n], sr_r.at[n], sibling).wait_recv()

    half = G // 2
    for t in range(T):
        for n in (0,) if t == 0 else (2 * t - 1, 2 * t):
            sib_wait(n)
        for h in (0, 1):

            def step(i, _):
                for way in (0, 1):
                    if t == 0 and h != way:
                        continue
                    n = 0 if t == 0 else 2 * t - 1 + way
                    arrived = t > 1 or (t == 1 and h == way)
                    if arrived:
                        pass_on(way, t - 1, i).wait_recv()
                    for image in range(IMG_DEV):
                        value = part(target(way, t), core * G + i, image)
                        value += sib_in[n, i, image].astype(F32)
                        if arrived:
                            value += rs_in[way, t - 1, i, image].astype(F32)
                        rs_out[way, t, i, image] = value.astype(BF16)
                    pass_on(way, t, i).start()
                return 0

            lax.fori_loop(h * half, (h + 1) * half, step, 0)

    def kvgrad_slot(j):
        return kvgrad_ref.at[:, :, :, head(j)]

    sib_wait(Z - 1)

    def finish(i, _):
        for way in (0, 1):
            pass_on(way, T - 1, i).wait_recv()
        for image in range(IMG_DEV):
            value = part(z, core * G + i, image) + sib_in[Z - 1, i, image].astype(F32)
            value += rs_in[0, T - 1, i, image].astype(F32) + rs_in[1, T - 1, i, image].astype(F32)
            fin_out[i, image] = value.astype(BF16)
        give(i, fin_out.at[i], kvgrad_slot, fin_s, fin_r)
        return 0

    lax.fori_loop(0, G, finish, 0)

    for i in range(G):
        given(i, kv_src(i), kv_s, kv_r)
        given(i, query_ref.at[:, head(i)], q_s, q_r)
        given(i, bias_ref, b_s, b_r)
        given(i, att_out.at[i], att_s, att_r)
        given(i, og_out.at[i], og_s, og_r)
        given(i, dq_out.at[i], dq_s, dq_r)
        given(i, fin_out.at[i], fin_s, fin_r)
        for way in (0, 1):
            for t in range(T):
                if in_step(way, t + 1, i):
                    ring_copy(way, t, z, i).wait_send()
                if t > 0 or (i < half) == (way == 0):
                    pass_on(way, t, i).wait_send()
    for n in range(Z):
        remote(half_block(z), half_block(z), sa_s.at[n], sa_r.at[n], sibling).wait_send()
        remote(sib_out.at[n], sib_in.at[n], sr_s.at[n], sr_r.at[n], sibling).wait_send()
    for k in range(1, M):
        remote(stat_out, stat_in.at[0], st_s.at[k], st_r.at[0], (dp, lax.rem(mp + k, M))).wait_send()
    block_copy.wait()
    normed_copy.wait()
    hgrad_copy.wait()
    for i in range(G):
        take(i, qgrad_slot, dq_s, dq_r)
        take(i, kvgrad_slot, fin_s, fin_r)


def local(
    Z,
    M,
    hidden_in,
    queries,
    image_kv,
    image_owner,
    citations,
    cite_mask,
    gate_scalars,
    norm_gain,
    upstream,
):
    width = hidden_in.shape[1]
    cites = cite_mask.shape[1]
    n_rows = Z * Y * IMG_DEV
    dp = lax.axis_index("dp")
    mp = lax.axis_index("mp")
    first = dp // Y * Y + mp % 2 * G
    ids = jnp.arange(n_rows, dtype=jnp.int32)
    cited_ids = lax.dynamic_slice_in_dim(citations, first, G, 0)
    rows = jnp.sum(jnp.where(cited_ids[:, :, None] == ids, image_owner, 0), axis=-1)
    places = cites - jnp.arange(cites, dtype=jnp.int32)
    pos = cites - jnp.max(
        jnp.where(rows[:, :, None] == ids, places[None, :, None], 0), axis=1
    )
    bias = jnp.where(cite_mask > 0, 0.0, -1e30).astype(F32).T
    gate = jnp.tanh(gate_scalars)
    gain = norm_gain.reshape(M, width)

    T = Z // 2
    smem = pl.BlockSpec(memory_space=pltpu.SMEM)
    vmem = pl.BlockSpec(memory_space=pltpu.VMEM)
    anywhere = pl.BlockSpec(memory_space=pl.ANY)
    heads = (G, TOK, HEAD_DIM)
    piece = (IMG_DEV, 2, IT, HEAD_DIM)
    keys = cites * IT
    dma = pltpu.SemaphoreType.DMA
    like = lambda v: jax.ShapeDtypeStruct(v.shape, v.dtype)
    return pl.pallas_call(
        functools.partial(kernel, Z, M, cites),
        out_shape=(like(hidden_in),) * 4 + (like(image_kv),),
        in_specs=[smem, smem, smem, anywhere, anywhere, anywhere, anywhere, vmem, anywhere],
        out_specs=(anywhere,) * 5,
        scratch_shapes=[
            pltpu.VMEM((n_rows, 2, IT, HEAD_DIM), BF16),
            pltpu.VMEM(heads, BF16),
            pltpu.VMEM((G, cites, TOK), F32),
            pltpu.VMEM((TOK, width), BF16),
            pltpu.VMEM((TOK, width), BF16),
            pltpu.VMEM((G, keys, HEAD_DIM), BF16),
            pltpu.VMEM((G, keys, HEAD_DIM), BF16),
            pltpu.VMEM((G, keys, TOK), F32),
            pltpu.VMEM(heads, BF16),
            pltpu.VMEM(heads, BF16),
            pltpu.VMEM((8, TOK), F32),
            pltpu.VMEM((M, 8, TOK), F32),
            pltpu.VMEM((TOK, width), BF16),
            pltpu.VMEM((TOK, width), BF16),
            pltpu.VMEM((TOK, width), BF16),
            pltpu.VMEM(heads, BF16),
            pltpu.VMEM(heads, BF16),
            pltpu.VMEM(heads, BF16),
            pltpu.VMEM((G, cites + 1, 2, IT, HEAD_DIM), F32),
            pltpu.VMEM((Z, G) + piece, BF16),
            pltpu.VMEM((Z, G) + piece, BF16),
            pltpu.VMEM((2, T, G) + piece, BF16),
            pltpu.VMEM((2, T, G) + piece, BF16),
            pltpu.VMEM((G,) + piece, BF16),
            dma((G,)),
            dma((G,)),
            dma((G,)),
            dma((G,)),
            dma((G,)),
            dma((G,)),
            dma((2, T, G)),
            dma((2, T, G)),
            dma((Z,)),
            dma((Z,)),
            dma((G,)),
            dma((G,)),
            dma((M,)),
            dma((M,)),
            dma((G,)),
            dma((G,)),
            dma((G,)),
            dma((G,)),
            dma((Z,)),
            dma((Z,)),
            dma((2, T, G)),
            dma((2, T, G)),
            dma((G,)),
            dma((G,)),
            dma((5,)),
        ],
        compiler_params=pltpu.CompilerParams(
            collective_id=0, has_side_effects=True, vmem_limit_bytes=48 * 1024 * 1024
        ),
        name="attend",
    )(
        rows.reshape(-1),
        pos.reshape(-1),
        gate,
        hidden_in,
        queries,
        image_kv,
        bias,
        gain,
        upstream,
    )


def solution(mesh):
    Z = mesh.shape["dp"] // Y
    M = mesh.shape["mp"]
    placed = (
        P("dp", "mp"),
        P("dp", "mp"),
        P("dp", None, None, "mp"),
        P(),
        P(),
        P("dp", None),
        P(),
        P(),
        P("dp", "mp"),
    )
    return jax.shard_map(
        functools.partial(local, Z, M),
        mesh=mesh,
        in_specs=placed,
        out_specs=(
            P("dp", "mp"),
            P("dp", "mp"),
            P("dp", "mp"),
            P("dp", "mp"),
            P("dp", None, None, "mp"),
        ),
        check_vma=False,
    )
```

time: 367 us -> 90.2 us (0.25)
  the two profiles are of different devices: /device:TPU:114 before, /device:TPU:1 now
where the time goes in v1:
time: 90.2 us; the launch traced here: 89.9 us
  Pallas kernels  80.5 us (89%)
  local copies, waits for them, and re-layouts  6.95 us (8%)
  between operations  1.47 us (2%)
  other arithmetic  1 us (1%)
    pallas_call x1, Pallas kernels, local(): pl.pallas_call(functools.partial(kernel, Z, M, cites), out_shape=(like(hi...  80.5 us
    unnamed x19, local copies, waits for them, and re-layouts  6.7 us

profile of v1, /device:TPU:1, one launch (start us, length us, event | category | flops | bytes accessed | tf_op | source)
XLA Modules:
  0.0 89.9 jit_solution(10610195154149137592)
XLA Ops:
  0.6 0.0 copy-start
  0.6 0.0 copy-start.1
  1.4 0.0 copy-done
  1.4 0.1 constant_dynamic-slice_fusion
  1.5 0.0 copy-start.5
  1.5 0.1 copy.15
  1.6 0.9 select_reduce_fusion.1
  2.5 0.1 reshape.26.rows_ref
  2.5 0.1 select_reduce_fusion
  2.7 0.0 copy-done.5
  2.7 0.0 copy-start.6
  2.7 0.7 copy-done.6
  3.4 0.0 copy-done.1
  3.4 0.0 copy-start.2
  3.4 0.9 %copy-done.2 = bf16[128,512]{1,0:T(8,128)(2,1)S(1)} copy-done((bf16[128,512]{1,0:T(8,128)(2,1)S(1)}, bf16[128,512]{1,0:T(8,128)(2,1)}, u32[]{:S(2)}) %copy-start.2) | copy-done | bytes 131096
  4.3 0.0 copy-start.3
  4.3 0.9 %copy-done.3 = bf16[2,2,32,512]{3,2,1,0:T(8,128)(2,1)S(1)} copy-done((bf16[2,2,32,512]{3,2,1,0:T(8,128)(2,1)S(1)}, bf16[2,2,32,512]{3,2,1,0:T(8,128)(2,1)}, u32[]{:S(2)}) %copy-start.3) | copy-done | bytes 131096
  5.2 0.9 %copy-done.4 = bf16[128,512]{1,0:T(8,128)(2,1)S(1)} copy-done((bf16[128,512]{1,0:T(8,128)(2,1)S(1)}, bf16[128,512]{1,0:T(8,128)(2,1)}, u32[]{:S(2)}) %copy-start.4) | copy-done | bytes 131096
  6.1 80.5 %attend.1 = (bf16[128,512]{1,0:T(8,128)(2,1)S(1)}, bf16[128,512]{1,0:T(8,128)(2,1)S(1)}, bf16[128,512]{1,0:T(8,128)(2,1)S(1)}, bf16[128,512]{1,0:T(8,128)(2,1)S(1)}, bf16[2,2,32,512]{3,2,1,0:T(8,128)(2,1)S(1)}) custom-call(s32[128]{0:T(128)S(1)} %reshape.26.rows_ref, s32[512]{0:T(512)S(1)} %subtract_bitcast_fusion.pos_ref, f32[1]{0:T(128)S(6)} %tanh.3.gate_ref, ...), custom_call_target="tpu_custom_call" | custom-call | tf_op jit(solution)/shard_map/attend/pallas_call | solution.py:478
  86.6 0.7 copy.22
  87.3 0.7 copy.23
  88.0 0.7 copy.24
  88.6 0.7 copy.25
  89.3 0.7 copy.26
  (5 shorter events, 0.0 us)
Async XLA Ops:
  0.6 0.8 copy-start
  0.6 2.8 %copy-start.1 = (bf16[128,512]{1,0:T(8,128)(2,1)S(1)}, bf16[128,512]{1,0:T(8,128)(2,1)}, u32[]{:S(2)}) copy-start(bf16[128,512]{1,0:T(8,128)(2,1)} %hidden_ref.1) | copy-start | bytes 393220
  1.5 1.2 %copy-start.5 = (s32[128,32]{0,1:T(8,128)S(1)}, s32[128,32]{0,1:T(8,128)}, u32[]{:S(2)}) copy-start(s32[128,32]{0,1:T(8,128)} %param.14) | copy-start | bytes 49156
  2.7 0.7 copy-start.6
  3.4 0.9 %copy-start.2 = (bf16[128,512]{1,0:T(8,128)(2,1)S(1)}, bf16[128,512]{1,0:T(8,128)(2,1)}, u32[]{:S(2)}) copy-start(bf16[128,512]{1,0:T(8,128)(2,1)} %query_ref.1) | copy-start | bytes 393220
  4.3 0.9 %copy-start.3 = (bf16[2,2,32,512]{3,2,1,0:T(8,128)(2,1)S(1)}, bf16[2,2,32,512]{3,2,1,0:T(8,128)(2,1)}, u32[]{:S(2)}) copy-start(bf16[2,2,32,512]{3,2,1,0:T(8,128)(2,1)} %kv_ref.1) | copy-start | bytes 393220
  5.2 0.9 %copy-start.4 = (bf16[128,512]{1,0:T(8,128)(2,1)S(1)}, bf16[128,512]{1,0:T(8,128)(2,1)}, u32[]{:S(2)}) copy-start(bf16[128,512]{1,0:T(8,128)(2,1)} %upstream_ref.1) | copy-start | bytes 393220

commit v2 on v1

--- a/solution.py
+++ b/solution.py
@@ -14,6 +14,7 @@
 Y = 8
 G = 4
 EPS = 1e-05
+VMEM_BYTES = 63 * 1024 * 1024
 MESH = pl.DeviceIdType.MESH
 F32 = jnp.float32
 BF16 = jnp.bfloat16
@@ -30,13 +31,13 @@
     Z,
     M,
     cites,
-    rows_ref,
-    pos_ref,
-    gate_ref,
     hidden_ref,
     query_ref,
     kv_ref,
-    bias_ref,
+    owner_ref,
+    citation_ref,
+    mask_ref,
+    gate_ref,
     gain_ref,
     upstream_ref,
     block_ref,
@@ -44,9 +45,15 @@
     hgrad_ref,
     qgrad_ref,
     kvgrad_ref,
+    owner,
+    citation,
+    gate_in,
+    gains,
+    pos_make,
+    pos,
     kv_all,
     q_all,
-    bias_all,
+    mask_all,
     hid,
     ups,
     ksel,
@@ -127,10 +134,18 @@
     def _():
         pl.semaphore_signal(barrier, inc=1, device_id=peer(b), device_id_type=MESH)
 
-    hid_copy = pltpu.make_async_copy(hidden_ref, hid, loc.at[0])
-    ups_copy = pltpu.make_async_copy(upstream_ref, ups, loc.at[1])
-    hid_copy.start()
-    ups_copy.start()
+    own_copies = []
+    for source, place in (
+        (citation_ref, citation),
+        (owner_ref, owner),
+        (gate_ref, gate_in),
+        (gain_ref, gains),
+        (hidden_ref, hid),
+        (upstream_ref, ups),
+    ):
+        copy = pltpu.make_async_copy(source, place, loc.at[len(own_copies)])
+        copy.start()
+        own_copies.append(copy)
 
     pl.semaphore_wait(barrier, (M - 1) + 2 + (G - 1) + jnp.where(in_group, 0, 1))
 
@@ -194,7 +209,7 @@
     for k in range(G):
         i = lax.rem(b + k, G)
         give(i, query_ref.at[:, head(i)], lambda j: q_all.at[j], q_s, q_r)
-        give(i, bias_ref, lambda j: bias_all.at[j], b_s, b_r)
+        give(i, mask_ref, lambda j: mask_all.at[j], b_s, b_r)
 
     def ring_copy(way, t, zb, i):
         block = piece(zb, core * G + i)
@@ -223,6 +238,26 @@
             if in_step(way, 1, i):
                 ring_copy(way, 0, z, i).start()
     to_sibling(0, z)
+
+    for copy in own_copies:
+        copy.wait()
+    first = z * Y + core * G
+
+    def row_of(s, n):
+        return owner[citation[n, first + s]]
+
+    lanes = lax.broadcasted_iota(jnp.int32, (8, n_rows), 1)
+    sublanes = lax.broadcasted_iota(jnp.int32, (8, n_rows), 0)
+
+    def place(n, found):
+        for s in range(G):
+            found = jnp.where((sublanes == s) & (lanes == row_of(s, n)), n, found)
+        return found
+
+    pos_make[...] = lax.fori_loop(0, cites, place, jnp.full((8, n_rows), cites, jnp.int32))
+    pos_copy = pltpu.make_async_copy(pos_make, pos, loc.at[9])
+    pos_copy.start()
+
     for t in range(1, T + 1):
         for i in range(G):
             for way in (0, 1):
@@ -241,18 +276,19 @@
         remote(other_half_block(zb), other_half_block(zb), sa_s.at[n], sa_r.at[n], sibling).wait_recv()
     for i in range(G):
         take(i, lambda j: q_all.at[j], q_s, q_r)
-        take(i, lambda j: bias_all.at[j], b_s, b_r)
+        take(i, lambda j: mask_all.at[j], b_s, b_r)
 
     scale = HEAD_DIM**-0.5
     log2e = 1.4426950408889634
 
     def forward(s, _):
         for n in range(cites):
-            row = rows_ref[s * cites + n]
+            row = row_of(s, n)
             ksel[s, n * IT : (n + 1) * IT] = kv_all[row, 0]
             vsel[s, n * IT : (n + 1) * IT] = kv_all[row, 1]
         scores = dot(ksel[s], q_all[s], NT) * (scale * log2e)
-        scores = scores.reshape(cites, IT, TOK) + bias_all[s][:, None, :]
+        scores = scores.reshape(cites, IT, TOK)
+        scores += jnp.where(mask_all[s] > 0, 0.0, -1e30).astype(F32)[:, None, :]
         top = jnp.max(jnp.max(scores, axis=0), axis=0, keepdims=True)
         weights = jnp.exp2(scores - top[None])
         total = jnp.sum(jnp.sum(weights, axis=0), axis=0, keepdims=True)
@@ -264,10 +300,8 @@
 
     lax.fori_loop(0, G, forward, 0)
 
-    gate = gate_ref[0]
-    hid_copy.wait()
-    ups_copy.wait()
-    gain = gain_ref[pl.ds(mp, 1), :]
+    gate = jnp.tanh(jnp.full((1, HEAD_DIM), gate_in[0], F32))
+    gain = [gains[pl.ds(mp * G + i, 1), :] for i in range(G)]
     square = jnp.zeros((TOK, HEAD_DIM), F32)
     inner = jnp.zeros((TOK, HEAD_DIM), F32)
     for i in range(G):
@@ -277,8 +311,8 @@
         mixed[:, lanes] = block
         wide = block.astype(F32)
         square += wide * wide
-        inner += gain[:, lanes] * ups[:, lanes].astype(F32) * wide
-    block_copy = pltpu.make_async_copy(mixed, block_ref, loc.at[2])
+        inner += gain[i] * ups[:, lanes].astype(F32) * wide
+    block_copy = pltpu.make_async_copy(mixed, block_ref, loc.at[6])
     block_copy.start()
     lane = lax.broadcasted_iota(jnp.int32, (TOK, HEAD_DIM), 1)
     both = jnp.where(
@@ -301,14 +335,14 @@
     for i in range(G):
         lanes = slice(i * HEAD_DIM, (i + 1) * HEAD_DIM)
         wide = mixed[:, lanes].astype(F32)
-        weighted = gain[:, lanes] * ups[:, lanes].astype(F32)
+        weighted = gain[i] * ups[:, lanes].astype(F32)
         grad = inverse * weighted - wide * slope
         og_out[i] = (gate * grad).astype(BF16)
         give(i, og_out.at[i], lambda j: og_in.at[j], og_s, og_r)
         hgrad[:, lanes] = grad.astype(BF16)
-        normed[:, lanes] = (wide * inverse * gain[:, lanes]).astype(BF16)
-    normed_copy = pltpu.make_async_copy(normed, normed_ref, loc.at[3])
-    hgrad_copy = pltpu.make_async_copy(hgrad, hgrad_ref, loc.at[4])
+        normed[:, lanes] = (wide * inverse * gain[i]).astype(BF16)
+    normed_copy = pltpu.make_async_copy(normed, normed_ref, loc.at[7])
+    hgrad_copy = pltpu.make_async_copy(hgrad, hgrad_ref, loc.at[8])
     normed_copy.start()
     hgrad_copy.start()
 
@@ -333,14 +367,15 @@
 
     def part(zb, yy, image):
         row = (zb * Y + yy) * IMG_DEV + image
-        total = cited[0, pos_ref[row]]
+        total = cited[0, pos[0, row]]
         for s in range(1, G):
-            total += cited[s, pos_ref[s * n_rows + row]]
+            total += cited[s, pos[s, row]]
         return total
 
     def target(way, t):
         return lax.rem(z + (T - t if way == 0 else Z - T + t), Z)
 
+    pos_copy.wait()
     order = [target(0, 0)]
     for t in range(1, T):
         order += [target(0, t), target(1, t)]
@@ -412,7 +447,7 @@
     for i in range(G):
         given(i, kv_src(i), kv_s, kv_r)
         given(i, query_ref.at[:, head(i)], q_s, q_r)
-        given(i, bias_ref, b_s, b_r)
+        given(i, mask_ref, b_s, b_r)
         given(i, att_out.at[i], att_s, att_r)
         given(i, og_out.at[i], og_s, og_r)
         given(i, dq_out.at[i], dq_s, dq_r)
@@ -436,6 +471,15 @@
         take(i, kvgrad_slot, fin_s, fin_r)
 
 
+def leave(*refs):
+    sources, places, sems = refs[:5], refs[5:10], refs[10]
+    copies = [pltpu.make_async_copy(s, p, sems.at[n]) for n, (s, p) in enumerate(zip(sources, places))]
+    for copy in copies:
+        copy.start()
+    for copy in copies:
+        copy.wait()
+
+
 def local(
     Z,
     M,
@@ -452,38 +496,28 @@
     width = hidden_in.shape[1]
     cites = cite_mask.shape[1]
     n_rows = Z * Y * IMG_DEV
-    dp = lax.axis_index("dp")
-    mp = lax.axis_index("mp")
-    first = dp // Y * Y + mp % 2 * G
-    ids = jnp.arange(n_rows, dtype=jnp.int32)
-    cited_ids = lax.dynamic_slice_in_dim(citations, first, G, 0)
-    rows = jnp.sum(jnp.where(cited_ids[:, :, None] == ids, image_owner, 0), axis=-1)
-    places = cites - jnp.arange(cites, dtype=jnp.int32)
-    pos = cites - jnp.max(
-        jnp.where(rows[:, :, None] == ids, places[None, :, None], 0), axis=1
-    )
-    bias = jnp.where(cite_mask > 0, 0.0, -1e30).astype(F32).T
-    gate = jnp.tanh(gate_scalars)
-    gain = norm_gain.reshape(M, width)
-
     T = Z // 2
-    smem = pl.BlockSpec(memory_space=pltpu.SMEM)
-    vmem = pl.BlockSpec(memory_space=pltpu.VMEM)
-    anywhere = pl.BlockSpec(memory_space=pl.ANY)
+    hbm = pl.BlockSpec(memory_space=pltpu.HBM)
     heads = (G, TOK, HEAD_DIM)
     piece = (IMG_DEV, 2, IT, HEAD_DIM)
     keys = cites * IT
     dma = pltpu.SemaphoreType.DMA
     like = lambda v: jax.ShapeDtypeStruct(v.shape, v.dtype)
-    return pl.pallas_call(
+    results = pl.pallas_call(
         functools.partial(kernel, Z, M, cites),
         out_shape=(like(hidden_in),) * 4 + (like(image_kv),),
-        in_specs=[smem, smem, smem, anywhere, anywhere, anywhere, anywhere, vmem, anywhere],
-        out_specs=(anywhere,) * 5,
+        in_specs=[hbm] * 9,
+        out_specs=(hbm,) * 5,
         scratch_shapes=[
+            pltpu.SMEM((n_rows,), jnp.int32),
+            pltpu.SMEM(citations.shape[::-1], jnp.int32),
+            pltpu.SMEM((1,), F32),
+            pltpu.VMEM((M * G, HEAD_DIM), F32),
+            pltpu.VMEM((8, n_rows), jnp.int32),
+            pltpu.SMEM((8, n_rows), jnp.int32),
             pltpu.VMEM((n_rows, 2, IT, HEAD_DIM), BF16),
             pltpu.VMEM(heads, BF16),
-            pltpu.VMEM((G, cites, TOK), F32),
+            pltpu.VMEM((G, cites, TOK), jnp.int32),
             pltpu.VMEM((TOK, width), BF16),
             pltpu.VMEM((TOK, width), BF16),
             pltpu.VMEM((G, keys, HEAD_DIM), BF16),
@@ -529,23 +563,32 @@
             dma((2, T, G)),
             dma((G,)),
             dma((G,)),
-            dma((5,)),
+            dma((10,)),
         ],
         compiler_params=pltpu.CompilerParams(
-            collective_id=0, has_side_effects=True, vmem_limit_bytes=48 * 1024 * 1024
+            collective_id=0, has_side_effects=True, vmem_limit_bytes=VMEM_BYTES
         ),
         name="attend",
     )(
-        rows.reshape(-1),
-        pos.reshape(-1),
-        gate,
         hidden_in,
         queries,
         image_kv,
-        bias,
-        gain,
+        image_owner,
+        citations.T,
+        cite_mask.T,
+        gate_scalars,
+        norm_gain.reshape(M * G, HEAD_DIM),
         upstream,
     )
+    return pl.pallas_call(
+        leave,
+        out_shape=tuple(like(v) for v in results),
+        in_specs=[hbm] * 5,
+        out_specs=(hbm,) * 5,
+        scratch_shapes=[dma((5,))],
+        compiler_params=pltpu.CompilerParams(vmem_limit_bytes=VMEM_BYTES),
+        name="leave",
+    )(*results)
 
 
 def solution(mesh):

time: 90.2 us -> 102 us (1.13)
  Pallas kernels: 80.5 us -> 101 us
  local copies, waits for them, and re-layouts: 6.95 us -> 0 us
    pallas_call x0 -> x1, Pallas kernels: none -> 21 us  [local(): pl.pallas_call(leave, out_shape=tuple((like(v) for v in results)), in_spe...]
    unnamed x19 -> x0, local copies, waits for them, and re-layouts: 6.7 us -> none
where the time goes in v2:
time: 102 us
  Pallas kernels  101 us (99%)
  between operations  1.29 us (1%)
    pallas_call x1, Pallas kernels, local(): pl.pallas_call(functools.partial(kernel, Z, M, cites), out_shape=(like(hi...  80 us
    pallas_call x1, Pallas kernels, local(): pl.pallas_call(leave, out_shape=tuple((like(v) for v in results)), in_spe...  21 us

profile of v2, /device:TPU:1, one launch (start us, length us, event | category | flops | bytes accessed | tf_op | source)
XLA Modules:
  0.0 102.3 jit_solution(2943991395497770066)
XLA Ops:
  1.3 80.0 %attend.1 = (bf16[128,512]{1,0:T(8,128)(2,1)}, bf16[128,512]{1,0:T(8,128)(2,1)}, bf16[128,512]{1,0:T(8,128)(2,1)}, bf16[128,512]{1,0:T(8,128)(2,1)}, bf16[2,2,32,512]{3,2,1,0:T(8,128)(2,1)}) custom-call(bf16[128,512]{1,0:T(8,128)(2,1)} %hidden_ref.1, bf16[128,512]{1,0:T(8,128)(2,1)} %query_ref.1, bf16[2,2,32,512]{3,2,1,0:T(8,128)(2,1)} %kv_ref.1, ...), custom_call_target="tpu_custom_call" | custom-call | tf_op jit(solution)/shard_map/attend/pallas_call | solution.py:506
  81.3 21.0 %leave.1 = (bf16[128,512]{1,0:T(8,128)(2,1)}, bf16[128,512]{1,0:T(8,128)(2,1)}, bf16[128,512]{1,0:T(8,128)(2,1)}, bf16[128,512]{1,0:T(8,128)(2,1)}, bf16[2,2,32,512]{3,2,1,0:T(8,128)(2,1)}) custom-call(bf16[128,512]{1,0:T(8,128)(2,1)} %get-tuple-element.10.refs_0_, bf16[128,512]{1,0:T(8,128)(2,1)} %get-tuple-element.11.refs_1_, ...), custom_call_target="tpu_custom_call" | custom-call | tf_op jit(solution)/shard_map/leave/pallas_call | solution.py:583

commit v3 on v0

v3 whole, which is shorter than its diff:
```python
import functools

import jax
import jax.numpy as jnp
from jax import lax
from jax.experimental import pallas as pl
from jax.experimental.pallas import tpu as pltpu
from jax.sharding import PartitionSpec as P

HEAD_DIM = 128
IT = 32
IMG_DEV = 2
TOK = 128
Y = 8
G = 4
EPS = 1e-05
VMEM_BYTES = 63 * 1024 * 1024
MESH = pl.DeviceIdType.MESH
F32 = jnp.float32
BF16 = jnp.bfloat16
NT = (((1,), (1,)), ((), ()))
TN = (((0,), (0,)), ((), ()))
NN = (((1,), (0,)), ((), ()))


def dot(left, right, dims):
    return lax.dot_general(left, right, dims, preferred_element_type=F32)


def kernel(
    Z,
    M,
    cites,
    hidden_ref,
    query_ref,
    kv_ref,
    owner_ref,
    citation_ref,
    mask_ref,
    gate_ref,
    gain_ref,
    upstream_ref,
    block_ref,
    normed_ref,
    hgrad_ref,
    qgrad_ref,
    kvgrad_ref,
    owner,
    citation,
    gate_in,
    gains,
    pos_make,
    pos,
    k_all,
    v_all,
    q_all,
    hid_all,
    ups_all,
    mask_all,
    ksel,
    vsel,
    probs,
    plow,
    plow_t,
    block_out,
    normed_out,
    hgrad_out,
    dq_out,
    out_grad,
    stat_out,
    stat_y,
    stat_x,
    cited,
    sums,
    sib_out,
    sib_in,
    rs_out,
    rs_in,
    fin_out,
    sent,
    kv_r,
    token_r,
    ag_r,
    sa_r,
    stat_r,
    out_r,
    sr_r,
    rs_r,
    loc,
):
    T = Z // 2
    X = M // 2
    kv_all = (k_all, v_all)
    n_rows = Z * Y * IMG_DEV
    feats = M * G * HEAD_DIM
    dp = lax.axis_index("dp")
    mp = lax.axis_index("mp")
    z, y = dp // Y, dp % Y
    x, core = mp // 2, mp % 2
    a, b = y // G, y % G
    right = (lax.rem(z + 1, Z) * Y + y, mp)
    left = (lax.rem(z + Z - 1, Z) * Y + y, mp)
    sibling = (dp, x * 2 + 1 - core)
    in_group = a == core

    def peer(i):
        return (z * Y + core * G + i, x * 2 + a)

    def y_peer(k):
        return (z * Y + lax.rem(y + k, Y), mp)

    def x_peer(k):
        return (dp, lax.rem(x + k, X) * 2 + core)

    barrier = pltpu.get_barrier_semaphore()
    others = [peer(lax.rem(b + k, G)) for k in range(1, G)] + [right, left, sibling]
    others += [y_peer(k) for k in range(1, Y)] + [x_peer(k) for k in range(1, X)]
    for other in others:
        pl.semaphore_signal(barrier, inc=1, device_id=other, device_id_type=MESH)

    @pl.when(jnp.logical_not(in_group))
    def _():
        pl.semaphore_signal(barrier, inc=1, device_id=peer(b), device_id_type=MESH)

    own_copies = []
    for source, place in (
        (citation_ref, citation),
        (owner_ref, owner),
        (gate_ref, gate_in),
        (gain_ref, gains),
    ):
        copy = pltpu.make_async_copy(source, place, loc.at[len(own_copies)])
        copy.start()
        own_copies.append(copy)

    pl.semaphore_wait(barrier, len(others) + jnp.where(in_group, 0, 1))

    def remote(src, dst, ssem, rsem, device):
        return pltpu.make_async_remote_copy(
            src_ref=src,
            dst_ref=dst,
            send_sem=ssem,
            recv_sem=rsem,
            device_id=device,
            device_id_type=MESH,
        )

    GROUP, RING, PAIR, STAT, SUM_RING, SUM_PAIR = range(6)

    def give(i, src, dst, rsem):
        mine = in_group & (i == b)

        @pl.when(mine)
        def _():
            pltpu.make_async_copy(src, dst, rsem).start()

        @pl.when(jnp.logical_not(mine))
        def _():
            remote(src, dst, sent.at[GROUP], rsem, peer(i)).start()

    def landed(buffer, rsem):
        pltpu.make_async_copy(buffer, buffer, rsem).wait()

    def left_here(buffer, kind):
        pltpu.make_async_copy(buffer, buffer, sent.at[kind]).wait()

    def head(i):
        return pl.ds(pl.multiple_of(i * HEAD_DIM, HEAD_DIM), HEAD_DIM)

    def kv_src(kv, i):
        return kv_ref.at[:, kv, :, head(i)]

    def piece(kv, zb, yy):
        return kv_all[kv].at[pl.ds((zb * Y + yy) * IMG_DEV, IMG_DEV)]

    turn = [lax.rem(b + k, G) for k in range(G)]
    for kv in (0, 1):
        for i in turn:
            give(i, kv_src(kv, i), piece(kv, z, y), kv_r.at[kv, b // 2])

    half_rows = G * IMG_DEV // 2

    def half_share(kv, zb, h):
        return kv_all[kv].at[pl.ds((zb * Y + core * G) * IMG_DEV + h * half_rows, half_rows)]

    def ring_copy(way, kv, t, zb, h):
        block = half_share(kv, zb, h)
        return remote(
            block,
            block,
            sent.at[RING],
            ag_r.at[way, kv, t, h],
            right if way == 0 else left,
        )

    def share(kv, zb, which):
        return kv_all[kv].at[pl.ds((zb * Y + which * G) * IMG_DEV, G * IMG_DEV)]

    def to_sibling(kv, zb):
        block = share(kv, zb, core)
        remote(block, block, sent.at[PAIR], sa_r.at[kv], sibling).start()

    def from_sibling(kv):
        landed(kv_all[kv].at[pl.ds(0, n_rows // 2)], sa_r.at[kv])

    def from_way(way, t):
        return lax.rem(z + (Z - t if way == 0 else t), Z)

    def in_step(way, t, h):
        return t < T or h == way

    for kv in (0, 1):
        for h in (0, 1):
            landed(half_share(kv, z, h), kv_r.at[kv, h])
            for way in (0, 1):
                if in_step(way, 1, h):
                    ring_copy(way, kv, 0, z, h).start()
        to_sibling(kv, z)

    token_inputs = (query_ref, q_all), (hidden_ref, hid_all), (upstream_ref, ups_all)
    for i in turn:
        give(i, mask_ref, mask_all.at[b], token_r.at[0])
    for n, (source, place) in enumerate(token_inputs):
        for i in turn:
            give(i, source.at[:, head(i)], place.at[b], token_r.at[min(n, 1)])

    for copy in own_copies:
        copy.wait()
    first = z * Y + core * G

    def row_of(s, n):
        return owner[citation[n, first + s]]

    lanes = lax.broadcasted_iota(jnp.int32, (8, n_rows), 1)
    sublanes = lax.broadcasted_iota(jnp.int32, (8, n_rows), 0)

    def find(n, found):
        for s in range(G):
            found = jnp.where((sublanes == s) & (lanes == row_of(s, n)), n, found)
        return found

    pos_make[...] = lax.fori_loop(0, cites, find, jnp.full((8, n_rows), cites, jnp.int32))
    pos_copy = pltpu.make_async_copy(pos_make, pos, loc.at[4])
    pos_copy.start()

    def ring_step(kv, t):
        for h in (0, 1):
            for way in (0, 1):
                if in_step(way, t, h):
                    zb = from_way(way, t)
                    ring_copy(way, kv, t - 1, zb, h).wait_recv()
                    if t < T and in_step(way, t + 1, h):
                        ring_copy(way, kv, t, zb, h).start()
        to_sibling(kv, from_way(0, t))
        if t < T:
            to_sibling(kv, from_way(1, t))

    for t in range(1, T):
        ring_step(0, t)
        ring_step(1, t)
    ring_step(0, T)
    from_sibling(0)
    landed(probs.at[:, pl.ds(0, 96)], token_r.at[0])

    scale = HEAD_DIM**-0.5
    log2e = 1.4426950408889634

    def scores_of(s, _):
        for n in range(cites):
            ksel[s, n * IT : (n + 1) * IT] = k_all[row_of(s, n)]
        scores = dot(ksel[s], q_all[s], NT) * (scale * log2e)
        scores = scores.reshape(cites, IT, TOK)
        scores += jnp.where(mask_all[s] > 0, 0.0, -1e30).astype(F32)[:, None, :]
        top = jnp.max(jnp.max(scores, axis=0), axis=0, keepdims=True)
        weights = jnp.exp2(scores - top[None])
        total = jnp.sum(jnp.sum(weights, axis=0), axis=0, keepdims=True)
        weights = (weights * (1.0 / total)[None]).reshape(cites * IT, TOK)
        probs[s] = weights
        rounded = weights.astype(BF16)
        plow[s] = rounded
        plow_t[s] = rounded.T
        return 0

    lax.fori_loop(0, G, scores_of, 0)

    ring_step(1, T)
    from_sibling(1)
    landed(probs.at[:, pl.ds(0, 128)], token_r.at[1])

    gate = jnp.tanh(jnp.full((1, HEAD_DIM), gate_in[0], F32))
    gain = gains[pl.ds(x * Y + y, 1), :]
    stat_lane = lax.broadcasted_iota(jnp.int32, (TOK, HEAD_DIM), 1)

    def attend(s, stats):
        for n in range(cites):
            vsel[s, n * IT : (n + 1) * IT] = v_all[row_of(s, n)]
        attended = dot(plow_t[s], vsel[s], NN)
        block = (hid_all[s].astype(F32) + gate * attended).astype(BF16)
        block_out[s] = block
        wide = block.astype(F32)
        square = jnp.sum(wide * wide, axis=1, keepdims=True)
        inner = jnp.sum(gain * ups_all[s].astype(F32) * wide, axis=1, keepdims=True)
        stats = jnp.where(stat_lane == 2 * s, square, stats)
        return jnp.where(stat_lane == 2 * s + 1, inner, stats)

    stats = lax.fori_loop(0, G, attend, jnp.zeros((TOK, HEAD_DIM), F32))

    stat_out[0] = jnp.transpose(stats)[:8]
    stat_y[y] = stat_out[0]
    for k in range(1, Y):
        remote(stat_out.at[0], stat_y.at[y], sent.at[STAT], stat_r.at[0], y_peer(k)).start()
    for s in range(G):
        give(s, block_out.at[s], block_ref.at[:, head(b)], out_r.at[0])
    landed(stat_y.at[pl.ds(0, Y - 1)], stat_r.at[0])
    total = stat_y[0]
    for k in range(1, Y):
        total += stat_y[k]
    stat_out[1] = total
    stat_x[x] = total
    for k in range(1, X):
        remote(stat_out.at[1], stat_x.at[x], sent.at[STAT], stat_r.at[1], x_peer(k)).start()
    if X > 1:
        landed(stat_x.at[pl.ds(0, X - 1)], stat_r.at[1])
    total = stat_x[0]
    for k in range(1, X):
        total += stat_x[k]
    columns = jnp.transpose(jnp.concatenate([total] * (TOK // 8), axis=0))

    for s in range(G):
        inverse = lax.rsqrt(columns[:, 2 * s : 2 * s + 1] / feats + EPS)
        slope = inverse * inverse * inverse * columns[:, 2 * s + 1 : 2 * s + 2] / feats
        wide = block_out[s].astype(F32)
        grad = inverse * (gain * ups_all[s].astype(F32)) - wide * slope
        out_grad[s] = (gate * grad).astype(BF16)
        hgrad_out[s] = grad.astype(BF16)
        normed_out[s] = (wide * inverse * gain).astype(BF16)
        cited[1, s, :cites] = dot(plow[s], out_grad[s], NN).reshape(cites, IT, HEAD_DIM)
        for kv in (0, 1):
            cited[kv, s, cites] = jnp.zeros((IT, HEAD_DIM), F32)

    def part(kv, row):
        total = cited[kv, 0, pos[0, row]]
        for s in range(1, G):
            total += cited[kv, s, pos[s, row]]
        return total

    def target(way, t):
        return lax.rem(z + (T - t if way == 0 else Z - T + t), Z)

    order = [target(0, 0)]
    for t in range(1, T):
        order += [target(0, t), target(1, t)]
    order += [z]

    def for_sibling(kv):
        for n, zb in enumerate(order):
            base = (zb * Y + (1 - core) * G) * IMG_DEV
            for r in range(G * IMG_DEV):
                sib_out[kv, n, r] = part(kv, base + r).astype(BF16)
            remote(
                sib_out.at[kv, n],
                sib_in.at[kv, n],
                sent.at[SUM_PAIR],
                sr_r.at[kv, min(n, 1)],
                sibling,
            ).start()

    def pass_on(way, kv, t, h):
        return remote(
            rs_out.at[way, kv, t, h],
            rs_in.at[way, kv, t, h],
            sent.at[SUM_RING],
            rs_r.at[way, kv, t, h],
            right if way == 0 else left,
        )

    def own(kv, n, r):
        base = (order[n] * Y + core * G) * IMG_DEV
        return part(kv, base + r) + sib_in[kv, n, r].astype(F32)

    def sum_start(kv):
        landed(sib_in.at[kv, 0], sr_r.at[kv, 0])
        for way in (0, 1):
            for r in range(half_rows):
                rs_out[way, kv, 0, way, r] = own(kv, 0, way * half_rows + r).astype(BF16)
            pass_on(way, kv, 0, way).start()
        landed(sib_in.at[kv, pl.ds(1, Z - 1)], sr_r.at[kv, 1])
        for n in range(1, Z):
            for r in range(G * IMG_DEV):
                sums[kv, n - 1, r] = own(kv, n, r)

    def sum_step(kv, t):
        for j in (0, 1):
            for way in (0, 1):
                h = j ^ way ^ 1 if t == 1 else j
                arrived = t > 1 or h == way
                if arrived:
                    pass_on(way, kv, t - 1, h).wait_recv()
                for r in range(half_rows):
                    value = sums[kv, 2 * t - 2 + way, h * half_rows + r]
                    if arrived:
                        value += rs_in[way, kv, t - 1, h, r].astype(F32)
                    rs_out[way, kv, t, h, r] = value.astype(BF16)
                pass_on(way, kv, t, h).start()

    def sum_end(kv):
        for h in (0, 1):
            for way in (0, 1):
                pass_on(way, kv, T - 1, h).wait_recv()
            for r in range(half_rows):
                value = sums[kv, Z - 2, h * half_rows + r]
                for way in (0, 1):
                    value += rs_in[way, kv, T - 1, h, r].astype(F32)
                fin_out[kv, h * half_rows + r] = value.astype(BF16)
            for i in range(h * G // 2, (h + 1) * G // 2):
                piece_out = fin_out.at[kv, pl.ds(i * IMG_DEV, IMG_DEV)]
                give(i, piece_out, kvgrad_ref.at[:, kv, :, head(b)], out_r.at[0])

    pos_copy.wait()
    for_sibling(1)
    sum_start(1)
    for s in range(G):
        give(s, hgrad_out.at[s], hgrad_ref.at[:, head(b)], out_r.at[0])
        give(s, normed_out.at[s], normed_ref.at[:, head(b)], out_r.at[0])

    def backward(s, _):
        weights = probs[s]
        prob_grad = dot(vsel[s], out_grad[s], NT)
        mean = jnp.sum(weights * prob_grad, axis=0, keepdims=True)
        score_grad = (weights * (prob_grad - mean) * scale).astype(BF16)
        cited[0, s, :cites] = dot(score_grad, q_all[s], NN).reshape(cites, IT, HEAD_DIM)
        dq_out[s] = dot(score_grad, ksel[s], TN).astype(BF16)
        return 0

    lax.fori_loop(0, G // 2, backward, 0)
    sum_step(1, 1)
    lax.fori_loop(G // 2, G, backward, 0)

    for_sibling(0)
    if T > 2:
        sum_step(1, 2)
    sum_start(0)
    for t in range(3, T):
        sum_step(1, t)
    for s in range(G):
        give(s, dq_out.at[s], qgrad_ref.at[:, head(b)], out_r.at[0])
    sum_step(0, 1)
    sum_end(1)
    for t in range(2, T):
        sum_step(0, t)
    sum_end(0)

    left_here(sib_in.at[:, pl.ds(0, Z - 1)], RING)
    left_here(sib_in, PAIR)
    left_here(stat_y.at[pl.ds(0, Y - 1)], STAT)
    if X > 1:
        left_here(stat_x.at[pl.ds(0, X - 1)], STAT)
    left_here(sib_in.at[:, pl.ds(0, Z - 1)], SUM_RING)
    left_here(sib_in, SUM_PAIR)
    group_rows = 304 * 2

    @pl.when(in_group)
    def _():
        left_here(probs.at[pl.ds(0, G - 1), pl.ds(0, group_rows)], GROUP)

    @pl.when(jnp.logical_not(in_group))
    def _():
        left_here(probs.at[:, pl.ds(0, group_rows)], GROUP)

    landed(probs.at[:, pl.ds(0, 160 * 2)], out_r.at[0])


def leave(*refs):
    sources, places, stages, sems = refs[:5], refs[5:10], refs[10:15], refs[15]
    loads = [
        pltpu.make_async_copy(s, p, sems.at[0, n]) for n, (s, p) in enumerate(zip(sources, stages))
    ]
    stores = [
        pltpu.make_async_copy(s, p, sems.at[1, n]) for n, (s, p) in enumerate(zip(stages, places))
    ]
    for copy in loads:
        copy.start()
    for load, store in zip(loads, stores):
        load.wait()
        store.start()
    for copy in stores:
        copy.wait()


def local(
    Z,
    M,
    hidden_in,
    queries,
    image_kv,
    image_owner,
    citations,
    cite_mask,
    gate_scalars,
    norm_gain,
    upstream,
):
    cites = cite_mask.shape[1]
    n_rows = Z * Y * IMG_DEV
    T = Z // 2
    hbm = pl.BlockSpec(memory_space=pltpu.HBM)
    heads = (G, TOK, HEAD_DIM)
    share = (G * IMG_DEV, IT, HEAD_DIM)
    half = (G * IMG_DEV // 2, IT, HEAD_DIM)
    keys = cites * IT
    dma = pltpu.SemaphoreType.DMA
    like = lambda v: jax.ShapeDtypeStruct(v.shape, v.dtype)
    results = pl.pallas_call(
        functools.partial(kernel, Z, M, cites),
        out_shape=(like(hidden_in),) * 4 + (like(image_kv),),
        in_specs=[hbm] * 9,
        out_specs=(hbm,) * 5,
        scratch_shapes=[
            pltpu.SMEM((n_rows,), jnp.int32),
            pltpu.SMEM(citations.shape[::-1], jnp.int32),
            pltpu.SMEM((1,), F32),
            pltpu.VMEM((M * G, HEAD_DIM), F32),
            pltpu.VMEM((8, n_rows), jnp.int32),
            pltpu.SMEM((8, n_rows), jnp.int32),
            pltpu.VMEM((n_rows, IT, HEAD_DIM), BF16),
            pltpu.VMEM((n_rows, IT, HEAD_DIM), BF16),
            pltpu.VMEM(heads, BF16),
            pltpu.VMEM(heads, BF16),
            pltpu.VMEM(heads, BF16),
            pltpu.VMEM((G, cites, TOK), jnp.int32),
            pltpu.VMEM((G, keys, HEAD_DIM), BF16),
            pltpu.VMEM((G, keys, HEAD_DIM), BF16),
            pltpu.VMEM((G, keys, TOK), F32),
            pltpu.VMEM((G, keys, TOK), BF16),
            pltpu.VMEM((G, TOK, keys), BF16),
            pltpu.VMEM(heads, BF16),
            pltpu.VMEM(heads, BF16),
            pltpu.VMEM(heads, BF16),
            pltpu.VMEM(heads, BF16),
            pltpu.VMEM(heads, BF16),
            pltpu.VMEM((2, 8, TOK), F32),
            pltpu.VMEM((Y, 8, TOK), F32),
            pltpu.VMEM((M // 2, 8, TOK), F32),
            pltpu.VMEM((2, G, cites + 1, IT, HEAD_DIM), F32),
            pltpu.VMEM((2, Z - 1) + share, F32),
            pltpu.VMEM((2, Z) + share, BF16),
            pltpu.VMEM((2, Z) + share, BF16),
            pltpu.VMEM((2, 2, T, 2) + half, BF16),
            pltpu.VMEM((2, 2, T, 2) + half, BF16),
            pltpu.VMEM((2,) + share, BF16),
            dma((6,)),
            dma((2, 2)),
            dma((2,)),
            dma((2, 2, T, 2)),
            dma((2,)),
            dma((2,)),
            dma((1,)),
            dma((2, 2)),
            dma((2, 2, T, 2)),
            dma((5,)),
        ],
        compiler_params=pltpu.CompilerParams(
            collective_id=0, has_side_effects=True, vmem_limit_bytes=VMEM_BYTES
        ),
        name="attend",
    )(
        hidden_in,
        queries,
        image_kv,
        image_owner,
        citations.T,
        cite_mask.T,
        gate_scalars,
        norm_gain.reshape(M * G, HEAD_DIM),
        upstream,
    )
    return pl.pallas_call(
        leave,
        out_shape=tuple(like(v) for v in results),
        in_specs=[hbm] * 5,
        out_specs=(hbm,) * 5,
        scratch_shapes=[pltpu.VMEM(v.shape, v.dtype) for v in results] + [dma((2, 5))],
        compiler_params=pltpu.CompilerParams(vmem_limit_bytes=VMEM_BYTES),
        name="leave",
    )(*results)


def solution(mesh):
    Z = mesh.shape["dp"] // Y
    M = mesh.shape["mp"]
    placed = (
        P("dp", "mp"),
        P("dp", "mp"),
        P("dp", None, None, "mp"),
        P(),
        P(),
        P("dp", None),
        P(),
        P(),
        P("dp", "mp"),
    )
    return jax.shard_map(
        functools.partial(local, Z, M),
        mesh=mesh,
        in_specs=placed,
        out_specs=(
            P("dp", "mp"),
            P("dp", "mp"),
            P("dp", "mp"),
            P("dp", "mp"),
            P("dp", None, None, "mp"),
        ),
        check_vma=False,
    )
```

time: 367 us -> 79.7 us (0.22)
  the two profiles are of different devices: /device:TPU:114 before, /device:TPU:1 now
where the time goes in v3:
time: 79.7 us; the launch traced here: 79.6 us
  Pallas kernels  78.3 us (98%)
  between operations  1.29 us (2%)
    pallas_call x1, Pallas kernels, local(): pl.pallas_call(functools.partial(kernel, Z, M, cites), out_shape=(like(hi...  76.4 us
    pallas_call x1, Pallas kernels, local(): pl.pallas_call(leave, out_shape=tuple((like(v) for v in results)), in_spe...  1.91 us

profile of v3, /device:TPU:1, one launch (start us, length us, event | category | flops | bytes accessed | tf_op | source)
XLA Modules:
  0.0 79.6 jit_solution(15573486776245068082)
XLA Ops:
  1.3 76.4 %attend.1 = (bf16[128,512]{1,0:T(8,128)(2,1)}, bf16[128,512]{1,0:T(8,128)(2,1)}, bf16[128,512]{1,0:T(8,128)(2,1)}, bf16[128,512]{1,0:T(8,128)(2,1)}, bf16[2,2,32,512]{3,2,1,0:T(8,128)(2,1)}) custom-call(bf16[128,512]{1,0:T(8,128)(2,1)} %hidden_ref.1, bf16[128,512]{1,0:T(8,128)(2,1)} %query_ref.1, bf16[2,2,32,512]{3,2,1,0:T(8,128)(2,1)} %kv_ref.1, ...), custom_call_target="tpu_custom_call" | custom-call | tf_op jit(solution)/shard_map/attend/pallas_call | solution.py:513
  77.7 1.9 %leave.1 = (bf16[128,512]{1,0:T(8,128)(2,1)}, bf16[128,512]{1,0:T(8,128)(2,1)}, bf16[128,512]{1,0:T(8,128)(2,1)}, bf16[128,512]{1,0:T(8,128)(2,1)}, bf16[2,2,32,512]{3,2,1,0:T(8,128)(2,1)}) custom-call(bf16[128,512]{1,0:T(8,128)(2,1)} %get-tuple-element.10.refs_0_, bf16[128,512]{1,0:T(8,128)(2,1)} %get-tuple-element.11.refs_1_, ...), custom_call_target="tpu_custom_call" | custom-call | tf_op jit(solution)/shard_map/leave/pallas_call | solution.py:577

commit v4 on v3

--- a/solution.py
+++ b/solution.py
@@ -68,9 +68,10 @@
     dq_out,
     out_grad,
     stat_out,
-    stat_y,
-    stat_x,
-    cited,
+    stat_in,
+    score_grad,
+    dense_k,
+    dense_v,
     sums,
     sib_out,
     sib_in,
@@ -106,15 +107,14 @@
     def peer(i):
         return (z * Y + core * G + i, x * 2 + a)
 
-    def y_peer(k):
-        return (z * Y + lax.rem(y + k, Y), mp)
-
-    def x_peer(k):
-        return (dp, lax.rem(x + k, X) * 2 + core)
+    far_first = sorted(range(1, X * Y), key=lambda k: -min(k % Y, Y - k % Y) - min(k // Y, X - k // Y))
+    head_peers = [
+        (z * Y + lax.rem(y + k % Y, Y), lax.rem(x + k // Y, X) * 2 + core) for k in far_first
+    ]
 
     barrier = pltpu.get_barrier_semaphore()
     others = [peer(lax.rem(b + k, G)) for k in range(1, G)] + [right, left, sibling]
-    others += [y_peer(k) for k in range(1, Y)] + [x_peer(k) for k in range(1, X)]
+    others += head_peers
     for other in others:
         pl.semaphore_signal(barrier, inc=1, device_id=other, device_id_type=MESH)
 
@@ -277,11 +277,12 @@
         weights = (weights * (1.0 / total)[None]).reshape(cites * IT, TOK)
         probs[s] = weights
         rounded = weights.astype(BF16)
-        plow[s] = rounded
+        plow[s, :cites] = rounded.reshape(cites, IT, TOK)
+        plow[s, cites] = jnp.zeros((IT, TOK), BF16)
         plow_t[s] = rounded.T
         return 0
 
-    lax.fori_loop(0, G, scores_of, 0)
+    lax.fori_loop(0, G, scores_of, 0, unroll=True)
 
     ring_step(1, T)
     from_sibling(1)
@@ -303,27 +304,32 @@
         stats = jnp.where(stat_lane == 2 * s, square, stats)
         return jnp.where(stat_lane == 2 * s + 1, inner, stats)
 
-    stats = lax.fori_loop(0, G, attend, jnp.zeros((TOK, HEAD_DIM), F32))
-
-    stat_out[0] = jnp.transpose(stats)[:8]
-    stat_y[y] = stat_out[0]
-    for k in range(1, Y):
-        remote(stat_out.at[0], stat_y.at[y], sent.at[STAT], stat_r.at[0], y_peer(k)).start()
+    stats = lax.fori_loop(0, G, attend, jnp.zeros((TOK, HEAD_DIM), F32), unroll=True)
+
+    stat_out[...] = jnp.transpose(stats)[:8]
+    slot = x * Y + y
+    stat_in[slot] = stat_out[...]
+    for other in head_peers:
+        remote(stat_out, stat_in.at[slot], sent.at[STAT], stat_r.at[0], other).start()
     for s in range(G):
         give(s, block_out.at[s], block_ref.at[:, head(b)], out_r.at[0])
-    landed(stat_y.at[pl.ds(0, Y - 1)], stat_r.at[0])
-    total = stat_y[0]
-    for k in range(1, Y):
-        total += stat_y[k]
-    stat_out[1] = total
-    stat_x[x] = total
-    for k in range(1, X):
-        remote(stat_out.at[1], stat_x.at[x], sent.at[STAT], stat_r.at[1], x_peer(k)).start()
-    if X > 1:
-        landed(stat_x.at[pl.ds(0, X - 1)], stat_r.at[1])
-    total = stat_x[0]
-    for k in range(1, X):
-        total += stat_x[k]
+
+    def order(n):
+        return lax.rem(z + T + Z + (-((n + 1) // 2) if n % 2 else n // 2), Z)
+
+    def spread(dense, source, which, n):
+        base = (order(n) * Y + (core if which else 1 - core) * G) * IMG_DEV
+        for r in range(G * IMG_DEV):
+            for s in range(G):
+                block = source[s, pos[s, base + r]]
+                dense[which, n, r * IT : (r + 1) * IT, s * TOK : (s + 1) * TOK] = block
+
+    pos_copy.wait()
+    for n in range(Z):
+        for which in (0, 1):
+            spread(dense_v, plow, which, n)
+    landed(stat_in.at[pl.ds(0, X * Y - 1)], stat_r.at[0])
+    total = jnp.sum(stat_in[...], axis=0)
     columns = jnp.transpose(jnp.concatenate([total] * (TOK // 8), axis=0))
 
     for s in range(G):
@@ -334,29 +340,17 @@
         out_grad[s] = (gate * grad).astype(BF16)
         hgrad_out[s] = grad.astype(BF16)
         normed_out[s] = (wide * inverse * gain).astype(BF16)
-        cited[1, s, :cites] = dot(plow[s], out_grad[s], NN).reshape(cites, IT, HEAD_DIM)
-        for kv in (0, 1):
-            cited[kv, s, cites] = jnp.zeros((IT, HEAD_DIM), F32)
-
-    def part(kv, row):
-        total = cited[kv, 0, pos[0, row]]
-        for s in range(1, G):
-            total += cited[kv, s, pos[s, row]]
-        return total
-
-    def target(way, t):
-        return lax.rem(z + (T - t if way == 0 else Z - T + t), Z)
-
-    order = [target(0, 0)]
-    for t in range(1, T):
-        order += [target(0, t), target(1, t)]
-    order += [z]
+
+    def dense_sum(kv, which, n):
+        tokens = (q_all, out_grad)[kv][...].reshape(G * TOK, HEAD_DIM)
+        left_side = (dense_k, dense_v)[kv][which, n]
+        return dot(left_side, tokens, NN).reshape(G * IMG_DEV, IT, HEAD_DIM)
 
     def for_sibling(kv):
-        for n, zb in enumerate(order):
-            base = (zb * Y + (1 - core) * G) * IMG_DEV
-            for r in range(G * IMG_DEV):
-                sib_out[kv, n, r] = part(kv, base + r).astype(BF16)
+        for n in range(Z):
+            if kv == 0:
+                spread(dense_k, score_grad, 0, n)
+            sib_out[kv, n] = dense_sum(kv, 0, n).astype(BF16)
             remote(
                 sib_out.at[kv, n],
                 sib_in.at[kv, n],
@@ -374,20 +368,22 @@
             right if way == 0 else left,
         )
 
-    def own(kv, n, r):
-        base = (order[n] * Y + core * G) * IMG_DEV
-        return part(kv, base + r) + sib_in[kv, n, r].astype(F32)
-
     def sum_start(kv):
+        if kv == 0:
+            spread(dense_k, score_grad, 1, 0)
+        value = dense_sum(kv, 1, 0)
         landed(sib_in.at[kv, 0], sr_r.at[kv, 0])
+        value = (value + sib_in[kv, 0].astype(F32)).astype(BF16)
         for way in (0, 1):
-            for r in range(half_rows):
-                rs_out[way, kv, 0, way, r] = own(kv, 0, way * half_rows + r).astype(BF16)
+            rs_out[way, kv, 0, way] = value[way * half_rows : (way + 1) * half_rows]
             pass_on(way, kv, 0, way).start()
+
+    def sum_own(kv):
         landed(sib_in.at[kv, pl.ds(1, Z - 1)], sr_r.at[kv, 1])
         for n in range(1, Z):
-            for r in range(G * IMG_DEV):
-                sums[kv, n - 1, r] = own(kv, n, r)
+            if kv == 0:
+                spread(dense_k, score_grad, 1, n)
+            sums[kv, n - 1] = dense_sum(kv, 1, n) + sib_in[kv, n].astype(F32)
 
     def sum_step(kv, t):
         for j in (0, 1):
@@ -416,45 +412,42 @@
                 piece_out = fin_out.at[kv, pl.ds(i * IMG_DEV, IMG_DEV)]
                 give(i, piece_out, kvgrad_ref.at[:, kv, :, head(b)], out_r.at[0])
 
-    pos_copy.wait()
     for_sibling(1)
-    sum_start(1)
-    for s in range(G):
-        give(s, hgrad_out.at[s], hgrad_ref.at[:, head(b)], out_r.at[0])
-        give(s, normed_out.at[s], normed_ref.at[:, head(b)], out_r.at[0])
 
     def backward(s, _):
         weights = probs[s]
         prob_grad = dot(vsel[s], out_grad[s], NT)
         mean = jnp.sum(weights * prob_grad, axis=0, keepdims=True)
-        score_grad = (weights * (prob_grad - mean) * scale).astype(BF16)
-        cited[0, s, :cites] = dot(score_grad, q_all[s], NN).reshape(cites, IT, HEAD_DIM)
-        dq_out[s] = dot(score_grad, ksel[s], TN).astype(BF16)
+        grad = (weights * (prob_grad - mean) * scale).astype(BF16)
+        score_grad[s, :cites] = grad.reshape(cites, IT, TOK)
+        score_grad[s, cites] = jnp.zeros((IT, TOK), BF16)
         return 0
 
-    lax.fori_loop(0, G // 2, backward, 0)
+    lax.fori_loop(0, G, backward, 0, unroll=True)
+    sum_start(1)
+
+    for_sibling(0)
+    sum_start(0)
+    sum_own(1)
+    for s in range(G):
+        give(s, hgrad_out.at[s], hgrad_ref.at[:, head(b)], out_r.at[0])
+        give(s, normed_out.at[s], normed_ref.at[:, head(b)], out_r.at[0])
     sum_step(1, 1)
-    lax.fori_loop(G // 2, G, backward, 0)
-
-    for_sibling(0)
-    if T > 2:
-        sum_step(1, 2)
-    sum_start(0)
-    for t in range(3, T):
+    sum_own(0)
+    sum_step(0, 1)
+    for s in range(G):
+        grad = score_grad[s, :cites].reshape(cites * IT, TOK)
+        dq_out[s] = dot(grad, ksel[s], TN).astype(BF16)
+        give(s, dq_out.at[s], qgrad_ref.at[:, head(b)], out_r.at[0])
+    for t in range(2, T):
         sum_step(1, t)
-    for s in range(G):
-        give(s, dq_out.at[s], qgrad_ref.at[:, head(b)], out_r.at[0])
-    sum_step(0, 1)
+        sum_step(0, t)
     sum_end(1)
-    for t in range(2, T):
-        sum_step(0, t)
     sum_end(0)
 
     left_here(sib_in.at[:, pl.ds(0, Z - 1)], RING)
     left_here(sib_in, PAIR)
-    left_here(stat_y.at[pl.ds(0, Y - 1)], STAT)
-    if X > 1:
-        left_here(stat_x.at[pl.ds(0, X - 1)], STAT)
+    left_here(stat_in.at[pl.ds(0, X * Y - 1)], STAT)
     left_here(sib_in.at[:, pl.ds(0, Z - 1)], SUM_RING)
     left_here(sib_in, SUM_PAIR)
     group_rows = 304 * 2
@@ -531,17 +524,18 @@
             pltpu.VMEM((G, keys, HEAD_DIM), BF16),
             pltpu.VMEM((G, keys, HEAD_DIM), BF16),
             pltpu.VMEM((G, keys, TOK), F32),
-            pltpu.VMEM((G, keys, TOK), BF16),
+            pltpu.VMEM((G, cites + 1, IT, TOK), BF16),
             pltpu.VMEM((G, TOK, keys), BF16),
             pltpu.VMEM(heads, BF16),
             pltpu.VMEM(heads, BF16),
             pltpu.VMEM(heads, BF16),
             pltpu.VMEM(heads, BF16),
             pltpu.VMEM(heads, BF16),
-            pltpu.VMEM((2, 8, TOK), F32),
-            pltpu.VMEM((Y, 8, TOK), F32),
-            pltpu.VMEM((M // 2, 8, TOK), F32),
-            pltpu.VMEM((2, G, cites + 1, IT, HEAD_DIM), F32),
+            pltpu.VMEM((8, TOK), F32),
+            pltpu.VMEM((M // 2 * Y, 8, TOK), F32),
+            pltpu.VMEM((G, cites + 1, IT, TOK), BF16),
+            pltpu.VMEM((2, Z, G * IMG_DEV * IT, G * TOK), BF16),
+            pltpu.VMEM((2, Z, G * IMG_DEV * IT, G * TOK), BF16),
             pltpu.VMEM((2, Z - 1) + share, F32),
             pltpu.VMEM((2, Z) + share, BF16),
             pltpu.VMEM((2, Z) + share, BF16),
@@ -553,7 +547,7 @@
             dma((2,)),
             dma((2, 2, T, 2)),
             dma((2,)),
-            dma((2,)),
+            dma((1,)),
             dma((1,)),
             dma((2, 2)),
             dma((2, 2, T, 2)),

time: 79.7 us -> 73.2 us (0.918)
  Pallas kernels: 78.3 us -> 71.8 us
    pallas_call x1, Pallas kernels: 76.4 us -> 69.9 us  [local(): pl.pallas_call(functools.partial(kernel, Z, M, cites), out_shape=(like(hi...]
where the time goes in v4:
time: 73.2 us; the launch traced here: 73.1 us
  Pallas kernels  71.8 us (98%)
  between operations  1.29 us (2%)
    pallas_call x1, Pallas kernels, local(): pl.pallas_call(functools.partial(kernel, Z, M, cites), out_shape=(like(hi...  69.9 us
    pallas_call x1, Pallas kernels, local(): pl.pallas_call(leave, out_shape=tuple((like(v) for v in results)), in_spe...  1.91 us

profile of v4, /device:TPU:1, one launch (start us, length us, event | category | flops | bytes accessed | tf_op | source)
XLA Modules:
  0.0 73.1 jit_solution(15369296269153355553)
XLA Ops:
  1.3 69.9 %attend.1 = (bf16[128,512]{1,0:T(8,128)(2,1)}, bf16[128,512]{1,0:T(8,128)(2,1)}, bf16[128,512]{1,0:T(8,128)(2,1)}, bf16[128,512]{1,0:T(8,128)(2,1)}, bf16[2,2,32,512]{3,2,1,0:T(8,128)(2,1)}) custom-call(bf16[128,512]{1,0:T(8,128)(2,1)} %hidden_ref.1, bf16[128,512]{1,0:T(8,128)(2,1)} %query_ref.1, bf16[2,2,32,512]{3,2,1,0:T(8,128)(2,1)} %kv_ref.1, ...), custom_call_target="tpu_custom_call" | custom-call | tf_op jit(solution)/shard_map/attend/pallas_call | solution.py:506
  71.2 1.9 %leave.1 = (bf16[128,512]{1,0:T(8,128)(2,1)}, bf16[128,512]{1,0:T(8,128)(2,1)}, bf16[128,512]{1,0:T(8,128)(2,1)}, bf16[128,512]{1,0:T(8,128)(2,1)}, bf16[2,2,32,512]{3,2,1,0:T(8,128)(2,1)}) custom-call(bf16[128,512]{1,0:T(8,128)(2,1)} %get-tuple-element.10.refs_0_, bf16[128,512]{1,0:T(8,128)(2,1)} %get-tuple-element.11.refs_1_, ...), custom_call_target="tpu_custom_call" | custom-call | tf_op jit(solution)/shard_map/leave/pallas_call | solution.py:571

commit v5 on v4

--- a/solution.py
+++ b/solution.py
@@ -77,6 +77,7 @@
     sib_in,
     rs_out,
     rs_in,
+    fin_sib,
     fin_out,
     sent,
     kv_r,
@@ -87,6 +88,7 @@
     out_r,
     sr_r,
     rs_r,
+    fs_r,
     loc,
 ):
     T = Z // 2
@@ -178,44 +180,37 @@
         for i in turn:
             give(i, kv_src(kv, i), piece(kv, z, y), kv_r.at[kv, b // 2])
 
-    half_rows = G * IMG_DEV // 2
-
-    def half_share(kv, zb, h):
-        return kv_all[kv].at[pl.ds((zb * Y + core * G) * IMG_DEV + h * half_rows, half_rows)]
-
-    def ring_copy(way, kv, t, zb, h):
-        block = half_share(kv, zb, h)
-        return remote(
-            block,
-            block,
-            sent.at[RING],
-            ag_r.at[way, kv, t, h],
-            right if way == 0 else left,
-        )
+    onward = (jnp.where(core == 0, right[0], left[0]), mp)
+    block_rows = Y * IMG_DEV
+    sub_rows = block_rows // 4
+    mine = [2 * core, 2 * core + 1]
+    theirs = [2 - 2 * core, 3 - 2 * core]
+
+    def sub_block(kv, zb, h):
+        return kv_all[kv].at[pl.ds(zb * block_rows + h * sub_rows, sub_rows)]
+
+    def ring_copy(kv, t, zb, h):
+        block = sub_block(kv, zb, h)
+        return remote(block, block, sent.at[RING], ag_r.at[kv, t, h], onward)
 
     def share(kv, zb, which):
         return kv_all[kv].at[pl.ds((zb * Y + which * G) * IMG_DEV, G * IMG_DEV)]
 
-    def to_sibling(kv, zb):
-        block = share(kv, zb, core)
-        remote(block, block, sent.at[PAIR], sa_r.at[kv], sibling).start()
+    def to_sibling(block, rsem):
+        remote(block, block, sent.at[PAIR], rsem, sibling).start()
 
     def from_sibling(kv):
-        landed(kv_all[kv].at[pl.ds(0, n_rows // 2)], sa_r.at[kv])
-
-    def from_way(way, t):
-        return lax.rem(z + (Z - t if way == 0 else t), Z)
-
-    def in_step(way, t, h):
-        return t < T or h == way
+        landed(kv_all[kv].at[pl.ds(0, (Z - 1) * G * IMG_DEV)], sa_r.at[1, kv])
 
     for kv in (0, 1):
         for h in (0, 1):
-            landed(half_share(kv, z, h), kv_r.at[kv, h])
-            for way in (0, 1):
-                if in_step(way, 1, h):
-                    ring_copy(way, kv, 0, z, h).start()
-        to_sibling(kv, z)
+            landed(sub_block(kv, z, mine[h]), kv_r.at[kv, h])
+            ring_copy(kv, 0, z, mine[h]).start()
+        to_sibling(share(kv, z, core), sa_r.at[0, kv])
+    for kv in (0, 1):
+        landed(share(kv, z, 1 - core), sa_r.at[0, kv])
+        for h in theirs:
+            ring_copy(kv, 0, z, h).start()
 
     token_inputs = (query_ref, q_all), (hidden_ref, hid_all), (upstream_ref, ups_all)
     for i in turn:
@@ -244,16 +239,15 @@
     pos_copy.start()
 
     def ring_step(kv, t):
-        for h in (0, 1):
-            for way in (0, 1):
-                if in_step(way, t, h):
-                    zb = from_way(way, t)
-                    ring_copy(way, kv, t - 1, zb, h).wait_recv()
-                    if t < T and in_step(way, t + 1, h):
-                        ring_copy(way, kv, t, zb, h).start()
-        to_sibling(kv, from_way(0, t))
+        zb = lax.rem(z + jnp.where(core == 0, Z - t, t), Z)
+        for n, h in enumerate(mine + theirs if t < T else mine):
+            ring_copy(kv, t - 1, zb, h).wait_recv()
+            if t < T - 1 or (t == T - 1 and n < 2):
+                ring_copy(kv, t, zb, h).start()
         if t < T:
-            to_sibling(kv, from_way(1, t))
+            to_sibling(kv_all[kv].at[pl.ds(zb * block_rows, block_rows)], sa_r.at[1, kv])
+        else:
+            to_sibling(share(kv, zb, core), sa_r.at[1, kv])
 
     for t in range(1, T):
         ring_step(0, t)
@@ -314,19 +308,22 @@
     for s in range(G):
         give(s, block_out.at[s], block_ref.at[:, head(b)], out_r.at[0])
 
-    def order(n):
-        return lax.rem(z + T + Z + (-((n + 1) // 2) if n % 2 else n // 2), Z)
+    def target(which, n):
+        to_right = (core == 0) if which else (core == 1)
+        return lax.rem(z + jnp.where(to_right, T - n, Z - T + n), Z)
 
     def spread(dense, source, which, n):
-        base = (order(n) * Y + (core if which else 1 - core) * G) * IMG_DEV
-        for r in range(G * IMG_DEV):
+        base = target(which, n) * block_rows
+        if n == 0:
+            base += (core if which else 1 - core) * (block_rows // 2)
+        for r in range(block_rows if n else block_rows // 2):
             for s in range(G):
                 block = source[s, pos[s, base + r]]
                 dense[which, n, r * IT : (r + 1) * IT, s * TOK : (s + 1) * TOK] = block
 
     pos_copy.wait()
-    for n in range(Z):
-        for which in (0, 1):
+    for n in range(T + 1):
+        for which in (0, 1) if n < T else (1,):
             spread(dense_v, plow, which, n)
     landed(stat_in.at[pl.ds(0, X * Y - 1)], stat_r.at[0])
     total = jnp.sum(stat_in[...], axis=0)
@@ -343,74 +340,82 @@
 
     def dense_sum(kv, which, n):
         tokens = (q_all, out_grad)[kv][...].reshape(G * TOK, HEAD_DIM)
-        left_side = (dense_k, dense_v)[kv][which, n]
-        return dot(left_side, tokens, NN).reshape(G * IMG_DEV, IT, HEAD_DIM)
+        rows = block_rows if n else block_rows // 2
+        left_side = (dense_k, dense_v)[kv][which, n, : rows * IT]
+        return dot(left_side, tokens, NN).reshape(rows, IT, HEAD_DIM)
 
     def for_sibling(kv):
-        for n in range(Z):
+        for n in range(T):
             if kv == 0:
                 spread(dense_k, score_grad, 0, n)
-            sib_out[kv, n] = dense_sum(kv, 0, n).astype(BF16)
+            rows = pl.ds(0, block_rows if n else block_rows // 2)
+            sib_out[kv, n, rows] = dense_sum(kv, 0, n).astype(BF16)
             remote(
-                sib_out.at[kv, n],
-                sib_in.at[kv, n],
+                sib_out.at[kv, n, rows],
+                sib_in.at[kv, n, rows],
                 sent.at[SUM_PAIR],
                 sr_r.at[kv, min(n, 1)],
                 sibling,
             ).start()
 
-    def pass_on(way, kv, t, h):
+    def pass_on(kv, t, h):
         return remote(
-            rs_out.at[way, kv, t, h],
-            rs_in.at[way, kv, t, h],
+            rs_out.at[kv, t, h],
+            rs_in.at[kv, t, h],
             sent.at[SUM_RING],
-            rs_r.at[way, kv, t, h],
-            right if way == 0 else left,
+            rs_r.at[kv, t, h],
+            onward,
         )
 
     def sum_start(kv):
         if kv == 0:
             spread(dense_k, score_grad, 1, 0)
         value = dense_sum(kv, 1, 0)
-        landed(sib_in.at[kv, 0], sr_r.at[kv, 0])
-        value = (value + sib_in[kv, 0].astype(F32)).astype(BF16)
-        for way in (0, 1):
-            rs_out[way, kv, 0, way] = value[way * half_rows : (way + 1) * half_rows]
-            pass_on(way, kv, 0, way).start()
+        landed(sib_in.at[kv, 0, pl.ds(0, block_rows // 2)], sr_r.at[kv, 0])
+        value = (value + sib_in[kv, 0, : block_rows // 2].astype(F32)).astype(BF16)
+        for h in (0, 1):
+            rs_out[kv, 0, h] = value[h * sub_rows : (h + 1) * sub_rows]
+            pass_on(kv, 0, h).start()
 
     def sum_own(kv):
-        landed(sib_in.at[kv, pl.ds(1, Z - 1)], sr_r.at[kv, 1])
-        for n in range(1, Z):
+        landed(sib_in.at[kv, pl.ds(1, T - 1)], sr_r.at[kv, 1])
+        for n in range(1, T + 1):
             if kv == 0:
                 spread(dense_k, score_grad, 1, n)
-            sums[kv, n - 1] = dense_sum(kv, 1, n) + sib_in[kv, n].astype(F32)
+            value = dense_sum(kv, 1, n)
+            sums[kv, n - 1] = value + sib_in[kv, n].astype(F32) if n < T else value
+
+    def with_arrived(kv, t, h, slot):
+        pass_on(kv, t - 1, slot).wait_recv()
+        return sums[kv, t - 1, pl.ds(h * sub_rows, sub_rows)] + rs_in[kv, t - 1, slot].astype(F32)
 
     def sum_step(kv, t):
-        for j in (0, 1):
-            for way in (0, 1):
-                h = j ^ way ^ 1 if t == 1 else j
-                arrived = t > 1 or h == way
-                if arrived:
-                    pass_on(way, kv, t - 1, h).wait_recv()
-                for r in range(half_rows):
-                    value = sums[kv, 2 * t - 2 + way, h * half_rows + r]
-                    if arrived:
-                        value += rs_in[way, kv, t - 1, h, r].astype(F32)
-                    rs_out[way, kv, t, h, r] = value.astype(BF16)
-                pass_on(way, kv, t, h).start()
+        for n, h in enumerate(theirs + mine):
+            if t == 1 and n < 2:
+                value = sums[kv, 0, pl.ds(h * sub_rows, sub_rows)]
+            else:
+                value = with_arrived(kv, t, h, n - 2 if t == 1 else h)
+            rs_out[kv, t, h] = value.astype(BF16)
+            pass_on(kv, t, h).start()
+
+    def last_exchange(kv):
+        return remote(fin_sib.at[0, kv], fin_sib.at[1, kv], sent.at[SUM_PAIR], fs_r.at[kv], sibling)
+
+    def sum_end_theirs(kv):
+        for n, h in enumerate(theirs):
+            value = with_arrived(kv, T, h, h).astype(BF16)
+            fin_sib[0, kv, n * sub_rows : (n + 1) * sub_rows] = value
+        last_exchange(kv).start()
 
     def sum_end(kv):
-        for h in (0, 1):
-            for way in (0, 1):
-                pass_on(way, kv, T - 1, h).wait_recv()
-            for r in range(half_rows):
-                value = sums[kv, Z - 2, h * half_rows + r]
-                for way in (0, 1):
-                    value += rs_in[way, kv, T - 1, h, r].astype(F32)
-                fin_out[kv, h * half_rows + r] = value.astype(BF16)
-            for i in range(h * G // 2, (h + 1) * G // 2):
-                piece_out = fin_out.at[kv, pl.ds(i * IMG_DEV, IMG_DEV)]
-                give(i, piece_out, kvgrad_ref.at[:, kv, :, head(b)], out_r.at[0])
+        values = [with_arrived(kv, T, h, h) for h in mine]
+        last_exchange(kv).wait_recv()
+        for n, value in enumerate(values):
+            rows = slice(n * sub_rows, (n + 1) * sub_rows)
+            fin_out[kv, rows] = (value + fin_sib[1, kv, rows].astype(F32)).astype(BF16)
+        for i in range(G):
+            piece_out = fin_out.at[kv, pl.ds(i * IMG_DEV, IMG_DEV)]
+            give(i, piece_out, kvgrad_ref.at[:, kv, :, head(b)], out_r.at[0])
 
     for_sibling(1)
 
@@ -442,14 +447,16 @@
     for t in range(2, T):
         sum_step(1, t)
         sum_step(0, t)
+    sum_end_theirs(1)
+    sum_end_theirs(0)
     sum_end(1)
     sum_end(0)
 
-    left_here(sib_in.at[:, pl.ds(0, Z - 1)], RING)
-    left_here(sib_in, PAIR)
+    left_here(k_all.at[pl.ds(0, (Z - 1) * block_rows)], RING)
+    left_here(k_all, PAIR)
     left_here(stat_in.at[pl.ds(0, X * Y - 1)], STAT)
-    left_here(sib_in.at[:, pl.ds(0, Z - 1)], SUM_RING)
-    left_here(sib_in, SUM_PAIR)
+    left_here(k_all.at[pl.ds(0, (Z - 1) * block_rows)], SUM_RING)
+    left_here(k_all, SUM_PAIR)
     group_rows = 304 * 2
 
     @pl.when(in_group)
@@ -499,7 +506,8 @@
     hbm = pl.BlockSpec(memory_space=pltpu.HBM)
     heads = (G, TOK, HEAD_DIM)
     share = (G * IMG_DEV, IT, HEAD_DIM)
-    half = (G * IMG_DEV // 2, IT, HEAD_DIM)
+    block = (Y * IMG_DEV, IT, HEAD_DIM)
+    quarter = (Y * IMG_DEV // 4, IT, HEAD_DIM)
     keys = cites * IT
     dma = pltpu.SemaphoreType.DMA
     like = lambda v: jax.ShapeDtypeStruct(v.shape, v.dtype)
@@ -534,23 +542,25 @@
             pltpu.VMEM((8, TOK), F32),
             pltpu.VMEM((M // 2 * Y, 8, TOK), F32),
             pltpu.VMEM((G, cites + 1, IT, TOK), BF16),
-            pltpu.VMEM((2, Z, G * IMG_DEV * IT, G * TOK), BF16),
-            pltpu.VMEM((2, Z, G * IMG_DEV * IT, G * TOK), BF16),
-            pltpu.VMEM((2, Z - 1) + share, F32),
-            pltpu.VMEM((2, Z) + share, BF16),
-            pltpu.VMEM((2, Z) + share, BF16),
-            pltpu.VMEM((2, 2, T, 2) + half, BF16),
-            pltpu.VMEM((2, 2, T, 2) + half, BF16),
+            pltpu.VMEM((2, T + 1, Y * IMG_DEV * IT, G * TOK), BF16),
+            pltpu.VMEM((2, T + 1, Y * IMG_DEV * IT, G * TOK), BF16),
+            pltpu.VMEM((2, T) + block, F32),
+            pltpu.VMEM((2, T) + block, BF16),
+            pltpu.VMEM((2, T) + block, BF16),
+            pltpu.VMEM((2, T, 4) + quarter, BF16),
+            pltpu.VMEM((2, T, 4) + quarter, BF16),
+            pltpu.VMEM((2, 2) + share, BF16),
             pltpu.VMEM((2,) + share, BF16),
             dma((6,)),
             dma((2, 2)),
             dma((2,)),
-            dma((2, 2, T, 2)),
-            dma((2,)),
+            dma((2, T, 4)),
+            dma((2, 2)),
             dma((1,)),
             dma((1,)),
             dma((2, 2)),
-            dma((2, 2, T, 2)),
+            dma((2, T, 4)),
+            dma((2,)),
             dma((5,)),
         ],
         compiler_params=pltpu.CompilerParams(

time: 73.2 us -> 70.6 us (0.964)
  Pallas kernels: 71.8 us -> 69.2 us
    pallas_call x1, Pallas kernels: 69.9 us -> 67.3 us  [local(): pl.pallas_call(functools.partial(kernel, Z, M, cites), out_shape=(like(hi...]
where the time goes in v5:
time: 70.6 us; the launch traced here: 70.5 us
  Pallas kernels  69.2 us (98%)
  between operations  1.29 us (2%)
    pallas_call x1, Pallas kernels, local(): pl.pallas_call(functools.partial(kernel, Z, M, cites), out_shape=(like(hi...  67.3 us
    pallas_call x1, Pallas kernels, local(): pl.pallas_call(leave, out_shape=tuple((like(v) for v in results)), in_spe...  1.91 us

profile of v5, /device:TPU:1, one launch (start us, length us, event | category | flops | bytes accessed | tf_op | source)
XLA Modules:
  0.0 70.5 jit_solution(3700107594813202188)
XLA Ops:
  1.3 67.3 %attend.1 = (bf16[128,512]{1,0:T(8,128)(2,1)}, bf16[128,512]{1,0:T(8,128)(2,1)}, bf16[128,512]{1,0:T(8,128)(2,1)}, bf16[128,512]{1,0:T(8,128)(2,1)}, bf16[2,2,32,512]{3,2,1,0:T(8,128)(2,1)}) custom-call(bf16[128,512]{1,0:T(8,128)(2,1)} %hidden_ref.1, bf16[128,512]{1,0:T(8,128)(2,1)} %query_ref.1, bf16[2,2,32,512]{3,2,1,0:T(8,128)(2,1)} %kv_ref.1, ...), custom_call_target="tpu_custom_call" | custom-call | tf_op jit(solution)/shard_map/attend/pallas_call | solution.py:514
  68.6 1.9 %leave.1 = (bf16[128,512]{1,0:T(8,128)(2,1)}, bf16[128,512]{1,0:T(8,128)(2,1)}, bf16[128,512]{1,0:T(8,128)(2,1)}, bf16[128,512]{1,0:T(8,128)(2,1)}, bf16[2,2,32,512]{3,2,1,0:T(8,128)(2,1)}) custom-call(bf16[128,512]{1,0:T(8,128)(2,1)} %get-tuple-element.10.refs_0_, bf16[128,512]{1,0:T(8,128)(2,1)} %get-tuple-element.11.refs_1_, ...), custom_call_target="tpu_custom_call" | custom-call | tf_op jit(solution)/shard_map/leave/pallas_call | solution.py:581

commit v6 on v5

--- a/solution.py
+++ b/solution.py
@@ -276,9 +276,9 @@
         plow_t[s] = rounded.T
         return 0
 
+    ring_step(1, T)
     lax.fori_loop(0, G, scores_of, 0, unroll=True)
 
-    ring_step(1, T)
     from_sibling(1)
     landed(probs.at[:, pl.ds(0, 128)], token_r.at[1])
 

time: 70.6 us -> 70.2 us (level)
  no operation moved by 1% of the time
where the time goes in v6:
time: 70.2 us; the launch traced here: 70.1 us
  Pallas kernels  68.8 us (98%)
  between operations  1.29 us (2%)
    pallas_call x1, Pallas kernels, local(): pl.pallas_call(functools.partial(kernel, Z, M, cites), out_shape=(like(hi...  66.9 us
    pallas_call x1, Pallas kernels, local(): pl.pallas_call(leave, out_shape=tuple((like(v) for v in results)), in_spe...  1.91 us

profile of v6, /device:TPU:1, one launch (start us, length us, event | category | flops | bytes accessed | tf_op | source)
XLA Modules:
  0.0 70.1 jit_solution(9600946283322662781)
XLA Ops:
  1.3 66.9 %attend.1 = (bf16[128,512]{1,0:T(8,128)(2,1)}, bf16[128,512]{1,0:T(8,128)(2,1)}, bf16[128,512]{1,0:T(8,128)(2,1)}, bf16[128,512]{1,0:T(8,128)(2,1)}, bf16[2,2,32,512]{3,2,1,0:T(8,128)(2,1)}) custom-call(bf16[128,512]{1,0:T(8,128)(2,1)} %hidden_ref.1, bf16[128,512]{1,0:T(8,128)(2,1)} %query_ref.1, bf16[2,2,32,512]{3,2,1,0:T(8,128)(2,1)} %kv_ref.1, ...), custom_call_target="tpu_custom_call" | custom-call | tf_op jit(solution)/shard_map/attend/pallas_call | solution.py:514
  68.2 1.9 %leave.1 = (bf16[128,512]{1,0:T(8,128)(2,1)}, bf16[128,512]{1,0:T(8,128)(2,1)}, bf16[128,512]{1,0:T(8,128)(2,1)}, bf16[128,512]{1,0:T(8,128)(2,1)}, bf16[2,2,32,512]{3,2,1,0:T(8,128)(2,1)}) custom-call(bf16[128,512]{1,0:T(8,128)(2,1)} %get-tuple-element.10.refs_0_, bf16[128,512]{1,0:T(8,128)(2,1)} %get-tuple-element.11.refs_1_, ...), custom_call_target="tpu_custom_call" | custom-call | tf_op jit(solution)/shard_map/leave/pallas_call | solution.py:581

commit v7 on v6

--- a/solution.py
+++ b/solution.py
@@ -443,6 +443,7 @@
     for s in range(G):
         grad = score_grad[s, :cites].reshape(cites * IT, TOK)
         dq_out[s] = dot(grad, ksel[s], TN).astype(BF16)
+    for s in range(G):
         give(s, dq_out.at[s], qgrad_ref.at[:, head(b)], out_r.at[0])
     for t in range(2, T):
         sum_step(1, t)

time: 70.2 us -> 70.1 us (level)
  no operation moved by 1% of the time
where the time goes in v7:
time: 70.1 us; the launch traced here: 70 us
  Pallas kernels  68.7 us (98%)
  between operations  1.29 us (2%)
    pallas_call x1, Pallas kernels, local(): pl.pallas_call(functools.partial(kernel, Z, M, cites), out_shape=(like(hi...  66.8 us
    pallas_call x1, Pallas kernels, local(): pl.pallas_call(leave, out_shape=tuple((like(v) for v in results)), in_spe...  1.91 us

profile of v7, /device:TPU:1, one launch (start us, length us, event | category | flops | bytes accessed | tf_op | source)
XLA Modules:
  0.0 70.0 jit_solution(18185372468031750349)
XLA Ops:
  1.3 66.8 %attend.1 = (bf16[128,512]{1,0:T(8,128)(2,1)}, bf16[128,512]{1,0:T(8,128)(2,1)}, bf16[128,512]{1,0:T(8,128)(2,1)}, bf16[128,512]{1,0:T(8,128)(2,1)}, bf16[2,2,32,512]{3,2,1,0:T(8,128)(2,1)}) custom-call(bf16[128,512]{1,0:T(8,128)(2,1)} %hidden_ref.1, bf16[128,512]{1,0:T(8,128)(2,1)} %query_ref.1, bf16[2,2,32,512]{3,2,1,0:T(8,128)(2,1)} %kv_ref.1, ...), custom_call_target="tpu_custom_call" | custom-call | tf_op jit(solution)/shard_map/attend/pallas_call | solution.py:515
  68.1 1.9 %leave.1 = (bf16[128,512]{1,0:T(8,128)(2,1)}, bf16[128,512]{1,0:T(8,128)(2,1)}, bf16[128,512]{1,0:T(8,128)(2,1)}, bf16[128,512]{1,0:T(8,128)(2,1)}, bf16[2,2,32,512]{3,2,1,0:T(8,128)(2,1)}) custom-call(bf16[128,512]{1,0:T(8,128)(2,1)} %get-tuple-element.10.refs_0_, bf16[128,512]{1,0:T(8,128)(2,1)} %get-tuple-element.11.refs_1_, ...), custom_call_target="tpu_custom_call" | custom-call | tf_op jit(solution)/shard_map/leave/pallas_call | solution.py:582
